TPU v7x, 32 devices: a whole 2x2x4 slice. The times are simulated.
32 devices in a mesh: parts: 2 (over y), chan: 4 (over z), tm: 2 (over x), rep: 2 (over core).
Axes of the slice: x: 2, y: 2, z: 4, core: 2. Of those that a mesh axis runs over, the one named last changes fastest.
Arguments:
- records: bfloat16 [64, 512, 512], P(('chan', 'tm', 'rep'), 'parts'), parts along dimension 1, may hold values from -6 to 6
- fir_taps: float32 [65], replicated, may hold values from -0.75 to 0.75
- source_ids: int32 [8], P('parts'), parts along dimension 0, may hold values from 0 to 3
Outputs:
- correlations: float32 [4, 512, 256], P(None, ('parts', 'chan')), parts along dimension 1
There are 2 independent parts, one for each index of `parts`. A program takes and returns all parts, laid end to end along the dimension named above; an argument that names none is the same for every part. Nothing has to cross between parts.
Inputs may be any that keep to these rules, and one draw needn't show every extreme that they name: `source_ids`: block indices along the segment, repeats allowed.
All inputs are finite; a program needn't handle non-finite values.
Results may differ from a plain program's by a relative error of at most 0.0074.
Values may be sent and summed in bfloat16 or wider, within the bound.
No kernel may reach another device: no remote copies, remote signals or barrier semaphores. Data moves between devices by JAX's collectives and lax.ppermute only.
A program may use at most 64 MiB of HBM per device.

v0:
```python
import math

import jax
import jax.numpy as jnp
from jax import lax
from jax.sharding import PartitionSpec as P

BINS = 96
LAGS = 256


def spread(value, axis, source):
    kept = jnp.where(lax.axis_index(axis) == source, value, 0).astype(value.dtype)
    return lax.psum(kept, axis)


def fir_matrix(fir_taps, samples):
    taps = fir_taps.shape[0]
    half = taps // 2
    rows = jnp.arange(samples)[:, None]
    cols = jnp.arange(samples)[None, :]
    offset = rows - cols + half
    inside = (offset >= 0) & (offset < taps)
    values = jnp.take(fir_taps, jnp.clip(offset, 0, taps - 1))
    return jnp.where(inside, values, jnp.float32(0.0)).astype(jnp.bfloat16)


def dft_table(samples, bins):
    times = jnp.arange(samples)[:, None]
    freqs = jnp.arange(1, bins + 1)[None, :]
    angle = 2.0 * math.pi / samples * (times * freqs % samples).astype(jnp.float32)
    return jnp.concatenate([jnp.cos(angle), -jnp.sin(angle)], axis=1).astype(jnp.bfloat16)


def lag_table(samples, bins, lags):
    freqs = jnp.arange(1, bins + 1)[:, None]
    shifts = jnp.arange(lags)[None, :] - lags // 2
    angle = 2.0 * math.pi / samples * jnp.mod(freqs * shifts, samples).astype(jnp.float32)
    return jnp.concatenate([jnp.cos(angle), -jnp.sin(angle)], axis=0)


def whiten(block, fir, dft, bins):
    filtered = jnp.einsum("wcs,st->wct", block, fir, preferred_element_type=jnp.float32).astype(
        jnp.bfloat16
    )
    spectra = jnp.einsum("wct,tf->wcf", filtered, dft, preferred_element_type=jnp.float32)
    real_part = spectra[..., :bins]
    imag_part = spectra[..., bins:]
    amp = jnp.sqrt(real_part * real_part + imag_part * imag_part)
    padded = jnp.pad(amp, ((0, 0), (0, 0), (2, 2)))
    smooth = (
        padded[..., 0:bins]
        + padded[..., 1 : bins + 1]
        + padded[..., 2 : bins + 2]
        + padded[..., 3 : bins + 3]
        + padded[..., 4 : bins + 4]
    ) / 5.0
    mean_amp = jnp.mean(amp, axis=-1, keepdims=True) + 1e-06
    level = jnp.maximum(smooth, 0.5 * mean_amp)
    return (spectra / jnp.concatenate([level, level], axis=-1)).astype(jnp.bfloat16)


def body(records, fir_taps, source_ids):
    samples = records.shape[2]
    fir = fir_matrix(fir_taps, samples)
    dft = dft_table(samples, BINS)
    count = source_ids.shape[0]
    local = lax.all_to_all(records, "chan", split_axis=1, concat_axis=0, tiled=True)
    white = whiten(local, fir, dft, BINS)
    pieces = []
    for index in range(count):
        remote = spread(white, "chan", source_ids[index])
        pieces.append(jnp.sum(remote, axis=1, dtype=jnp.float32))
    source = jnp.stack(pieces, axis=0)
    windows_here, block_width, unused_bins = white.shape
    white_re = white[..., :BINS].astype(jnp.float32)[None]
    white_im = white[..., BINS:].astype(jnp.float32)[None]
    src_re = source[..., :BINS][:, :, None, :]
    src_im = source[..., BINS:][:, :, None, :]
    cross_re = jnp.sum(white_re * src_re + white_im * src_im, axis=1)
    cross_im = jnp.sum(white_im * src_re - white_re * src_im, axis=1)
    cross = jnp.concatenate([cross_re, cross_im], axis=-1)
    table = lag_table(samples, BINS, LAGS)
    windows_all = windows_here * lax.axis_size("tm") * lax.axis_size("rep")
    scale = 1.0 / math.sqrt(windows_all * block_width * BINS)
    partial_lags = scale * jnp.einsum("scf,fl->scl", cross, table, precision=lax.Precision.HIGHEST)
    return lax.psum(partial_lags, ("tm", "rep"))


def solution(mesh):
    in_specs = (P(("chan", "tm", "rep"), "parts", None), P(), P("parts"))
    out_specs = P(None, ("parts", "chan"), None)
    return jax.shard_map(body, mesh=mesh, in_specs=in_specs, out_specs=out_specs, check_vma=False)
```

profile of v0, /device:TPU:0, one launch (start us, length us, event | category | flops | bytes accessed | tf_op | source)
XLA Modules:
  0.0 1683.0 jit_solution(6366929803698799162)
XLA Ops:
  6.5 0.0 copy-start
  6.5 3.1 copy.8
  9.6 6.3 all-to-all-start
  15.9 0.0 all-reduce.7.cloned.1.call-start
  15.9 0.2 fusion.2
  16.1 0.3 copy.11
  16.4 0.1 broadcast_clamp_fusion
  16.5 0.0 copy-done
  16.6 1522.5 %gather_fusion = bf16[262144]{0:T(1024)(128)(2,1)S(1)} fusion(f32[65]{0:T(128)S(1)} %copy-done, s32[262144]{0:T(1024)S(1)} %broadcast_clamp_fusion), kind=kCustom, calls=%fused_computation | custom fusion | bytes 2097152 | tf_op jit(solution)/shard_map/jit(_take)/gather | solution.py:24
  1539.1 0.0 copy-start.3
  1539.1 0.3 reshape.81
  1539.4 0.3 copy-done.3
  1539.7 0.6 fusion.59
  1542.9 0.9 cosine_convert_fusion
  1543.7 0.0 all-to-all-done
  1543.8 1.4 copy.9
  1545.2 0.1 copy.10
  1545.3 1.2 fusion.1
  1546.5 0.4 fusion.56
  1546.9 0.7 multiply_maximum_fusion
  1547.6 1.2 broadcast_select_fusion.3
  1548.8 1.2 broadcast_select_fusion.2
  1550.0 0.0 all-reduce.7.cloned.1.call-update
  1550.1 0.0 all-reduce.5.cloned.1.call-start
  1550.1 0.5 fusion.40
  1550.6 0.2 slice_convert_fusion.1
  1550.8 89.0 %all-reduce.7.cloned.1.call-done = (bf16[16,64,192]{2,1,0:T(8,128)(2,1)}, bf16[16,64,192]{2,1,0:T(8,128)(2,1)}, bf16[16,64,192]{2,1,0:T(8,128)(2,1)}, bf16[16,64,192]{2,1,0:T(8,128)(2,1)}) async-done(((bf16[16,64,192]{2,1,0:T(8,128)(2,1)}, bf16[16,64,192]{2,1,0:T(8,128)(2,1)}, bf16[16,64,192]{2,1,0:T(8,128)(2,1)}, bf16[16,64,192]{2,1,0:T(8,128)(2,1)}), (bf16[16,64,192]{2,1,0:T(8,128)(2,1)}, ...) | async-done | bytes 1572880 | tf_op jit(solution)/shard_map/psum | solution.py:14
  1639.7 0.0 copy-start.1
  1639.7 0.0 copy-start.2
  1639.7 1.5 convert_reduce_fusion.2
  1641.3 0.0 copy-done.1
  1641.3 0.0 copy-done.2
  1641.3 0.2 convert_reduce_fusion
  1641.5 0.1 fusion.58
  1641.6 0.7 add_reduce_fusion
  1642.3 1.1 convolution_multiply_fusion
  1643.5 0.0 all-reduce.5.cloned.1.call-update
  1643.5 31.0 %all-reduce.5.cloned.1.call-done = f32[4,64,256]{2,1,0:T(8,128)} async-done(((f32[4,64,256]{2,1,0:T(8,128)}), f32[4,64,256]{2,1,0:T(8,128)}) %all-reduce.5.cloned.1.call-update) | async-done | bytes 262160 | tf_op jit(solution)/shard_map/psum | solution.py:87
  1674.5 1.7 copy.17
  (4 shorter events, 0.0 us)
Async XLA Ops:
  6.5 10.0 copy-start
  9.6 1534.1 %all-to-all-start = ((bf16[4,256,512]{2,0,1:T(4,128)(2,1)}), bf16[4,256,512]{2,0,1:T(4,128)(2,1)}, u32[]{:S(2)}, u32[]{:S(2)}) async-start(bf16[4,256,512]{2,0,1:T(4,128)(2,1)} %copy.8), calls=%async_computation | async-start | bytes 2097152 | tf_op jit(solution)/shard_map/all_to_all | solution.py:68
  15.9 1623.8 %all-reduce.7.cloned.1.call-start = ((), (), s32[]{:S(2)}) async-start(), calls=%async_computation.2 | async-start | bytes 4194304 | tf_op jit(solution)/shard_map/psum | solution.py:14
  1539.1 0.7 copy-start.3
  1550.1 124.5 %all-reduce.5.cloned.1.call-start = ((), (), s32[]{:S(2)}) async-start(), calls=%async_computation.1 | async-start | bytes 524288 | tf_op jit(solution)/shard_map/psum | solution.py:87
  1639.7 1.5 copy-start.1
  1639.7 1.5 copy-start.2
Sparse Core Ops, SparseCore 0:
  1550.2 89.5 all-reduce.6
  1643.6 30.8 all-reduce.4
where the time goes:
time: 1680 us
  local copies, waits for them, and re-layouts  1530 us (91%)
  waiting for transfers between devices  120 us (7%)
    gather x2, local copies, waits for them, and re-layouts, fir_matrix(): values = jnp.take(fir_taps, jnp.clip(offset, 0, taps - 1))  1520 us
    psum x1, waiting for transfers between devices, spread(): return lax.psum(kept, axis)  89 us
  transfers between devices with their start and end apart: 3, of which 2 were waited for; matrix products, arithmetic and copies ran while one was open for 91% of the time, Pallas kernels for 0%

commit v1 on v0

v1 whole, which is shorter than its diff:
```python
import functools
import math

import jax
import jax.numpy as jnp
import numpy as np
from jax import lax
from jax.experimental import pallas as pl
from jax.experimental.pallas import tpu as pltpu
from jax.sharding import PartitionSpec as P

BINS = 96
LAGS = 256
BLOCK = 64
LANES = 128
VMEM_LIMIT = 32 * 1024 * 1024


def dft_table(samples):
    times = np.arange(samples)[:, None]
    freqs = np.arange(1, BINS + 1)[None, :]
    angle = np.float32(2.0 * math.pi / samples) * (times * freqs % samples).astype(np.float32)
    table = np.zeros((samples, 2 * LANES), np.float32)
    table[:, :BINS] = np.cos(angle)
    table[:, LANES : LANES + BINS] = -np.sin(angle)
    return table.astype(jnp.bfloat16)


def lag_table(samples):
    freqs = np.arange(1, BINS + 1)[:, None]
    shifts = np.arange(LAGS)[None, :] - LAGS // 2
    angle = np.float32(2.0 * math.pi / samples) * np.mod(freqs * shifts, samples).astype(np.float32)
    table = np.zeros((2 * LANES, LAGS), np.float32)
    table[:BINS] = np.cos(angle)
    table[LANES : LANES + BINS] = -np.sin(angle)
    high = table.astype(jnp.bfloat16)
    low = (table - high.astype(np.float32)).astype(jnp.bfloat16)
    return np.concatenate([high, low], axis=0)


def fir_blocks(taps_ref, pad_ref):
    taps = taps_ref.shape[1]
    half = taps // 2
    pad_ref[...] = jnp.zeros(pad_ref.shape, jnp.float32)
    pad_ref[0:1, 0:taps] = taps_ref[...]
    rows = lax.broadcasted_iota(jnp.int32, (LANES, LANES), 0)
    cols = lax.broadcasted_iota(jnp.int32, (LANES, LANES), 1)
    flip = (rows + cols == taps - 1).astype(jnp.bfloat16)
    turned = jnp.dot(
        pad_ref[...].astype(jnp.bfloat16), flip, preferred_element_type=jnp.float32
    )[0:1]
    wide = jnp.concatenate([turned, jnp.zeros((1, 2 * LANES), jnp.float32)], axis=1)
    wide = jnp.broadcast_to(wide, (LANES, 3 * LANES))
    return pltpu.roll(wide, LANES - half, 1, stride=1, stride_axis=0)


def pack(re, im):
    lane = lax.broadcasted_iota(jnp.int32, re[0].shape, 1)
    tiles = []
    for index in range(3):
        for part, last in ((re[index], re[3]), (im[index], im[3])):
            moved = pltpu.roll(last, BINS - 32 * index, 1)
            tiles.append(jnp.where(lane < BINS, part, moved))
    return jnp.concatenate(tiles, axis=1)


def unpack(packed):
    lane = lax.broadcasted_iota(jnp.int32, (packed.shape[0], LANES), 1)
    tiles = [packed[:, LANES * i : LANES * (i + 1)] for i in range(6)]
    last = []
    for which in range(2):
        total = jnp.zeros_like(tiles[0])
        for index in range(3):
            moved = pltpu.roll(tiles[2 * index + which], LANES - BINS + 32 * index, 1)
            total = jnp.where((lane >= 32 * index) & (lane < 32 * index + 32), moved, total)
        last.append(total)
    rows = [jnp.concatenate([tiles[2 * i], tiles[2 * i + 1]], axis=1) for i in range(3)]
    return jnp.concatenate(rows + [jnp.concatenate(last, axis=1)], axis=0)


def spectra_kernel(me_ref, ids_ref, rec_ref, taps_ref, dft_ref, out_ref, pad, fir, white, sums):
    windows, channels, samples = rec_ref.shape
    blocks = channels // BLOCK
    count = ids_ref.shape[0]
    three = fir_blocks(taps_ref, pad).astype(jnp.bfloat16)
    fir[...] = jnp.zeros(fir.shape, fir.dtype)
    tiles = samples // LANES
    for i in range(tiles):
        for j in range(max(i - 1, 0), min(i + 2, tiles)):
            fir[LANES * i : LANES * (i + 1), LANES * j : LANES * (j + 1)] = three[
                :, LANES * (j - i + 1) : LANES * (j - i + 2)
            ]
    for b in range(blocks):
        rows = rec_ref[:, BLOCK * b : BLOCK * (b + 1), :].reshape(windows * BLOCK, samples)
        filtered = jnp.dot(rows, fir[...], preferred_element_type=jnp.float32).astype(jnp.bfloat16)
        spectra = jnp.dot(filtered, dft_ref[...], preferred_element_type=jnp.float32)
        re, im = spectra[:, :LANES], spectra[:, LANES:]
        amp = jnp.sqrt(re * re + im * im)
        pair = amp + pltpu.roll(amp, 1, 1)
        smooth = (pltpu.roll(pair, LANES - 2, 1) + pair + pltpu.roll(amp, 2, 1)) / 5.0
        mean_amp = jnp.sum(amp, axis=1, keepdims=True) / BINS + 1e-06
        level = jnp.maximum(smooth, 0.5 * mean_amp)
        scale = 1.0 / level
        for which, value in enumerate((re, im)):
            unit = (value * scale).astype(jnp.bfloat16)
            white[which, b] = unit.reshape(windows, BLOCK, LANES)
            sums[which, b] = jnp.sum(
                unit.astype(jnp.float32).reshape(windows, BLOCK, LANES), axis=1
            )
    for k in range(blocks):
        b = lax.rem(me_ref[0] + k, blocks)
        re, im = [], []
        for s in range(count):
            total_re = jnp.zeros((BLOCK, LANES), jnp.float32)
            total_im = jnp.zeros((BLOCK, LANES), jnp.float32)
            for w in range(windows):
                src_re = sums[0, ids_ref[s], w : w + 1, :]
                src_im = sums[1, ids_ref[s], w : w + 1, :]
                white_re = white[0, b, w].astype(jnp.float32)
                white_im = white[1, b, w].astype(jnp.float32)
                total_re += white_re * src_re + white_im * src_im
                total_im += white_im * src_re - white_re * src_im
            re.append(total_re)
            im.append(total_im)
        out_ref[BLOCK * k : BLOCK * (k + 1), :] = pack(re, im).astype(jnp.bfloat16)


def local_cross(me, source_ids, records, taps, dft):
    windows, channels, samples = records.shape
    blocks = channels // BLOCK
    vmem = pl.BlockSpec(memory_space=pltpu.VMEM)
    smem = pl.BlockSpec(memory_space=pltpu.SMEM)
    return pl.pallas_call(
        spectra_kernel,
        out_shape=jax.ShapeDtypeStruct((channels, 6 * LANES), jnp.bfloat16),
        in_specs=[smem, smem, vmem, vmem, vmem],
        out_specs=vmem,
        scratch_shapes=[
            pltpu.VMEM((8, LANES), jnp.float32),
            pltpu.VMEM((samples, samples), jnp.bfloat16),
            pltpu.VMEM((2, blocks, windows, BLOCK, LANES), jnp.bfloat16),
            pltpu.VMEM((2, blocks, windows, LANES), jnp.float32),
        ],
        compiler_params=pltpu.CompilerParams(vmem_limit_bytes=VMEM_LIMIT),
    )(me, source_ids, records, taps, dft)


def add_kernel(pieces, *refs):
    inputs, outputs = refs[: len(refs) - pieces], refs[len(refs) - pieces :]
    rows = outputs[0].shape[0]
    for k, out in enumerate(outputs):
        at = slice(rows * k, rows * (k + 1))
        total = inputs[0][at, :].astype(jnp.float32)
        for ref in inputs[1:]:
            total += ref[at, :].astype(jnp.float32)
        out[...] = total.astype(out.dtype)


def added(arrays, pieces):
    rows, width = arrays[0].shape
    vmem = pl.BlockSpec(memory_space=pltpu.VMEM)
    return pl.pallas_call(
        functools.partial(add_kernel, pieces),
        out_shape=[jax.ShapeDtypeStruct((rows // pieces, width), jnp.bfloat16)] * pieces,
        in_specs=[vmem] * len(arrays),
        out_specs=[vmem] * pieces,
        compiler_params=pltpu.CompilerParams(vmem_limit_bytes=VMEM_LIMIT),
    )(*arrays)


def gather_kernel(core_ref, *refs):
    own, first, rest, out = refs[0], refs[1], refs[2:-1], refs[-1]
    total = jnp.where(core_ref[0] == 0, own[...].astype(jnp.float32), first[...].astype(jnp.float32))
    for ref in rest:
        total += ref[...].astype(jnp.float32)
    out[...] = total.astype(out.dtype)


def gathered(core, arrays):
    vmem = pl.BlockSpec(memory_space=pltpu.VMEM)
    smem = pl.BlockSpec(memory_space=pltpu.SMEM)
    return pl.pallas_call(
        gather_kernel,
        out_shape=jax.ShapeDtypeStruct(arrays[0].shape, jnp.bfloat16),
        in_specs=[smem] + [vmem] * len(arrays),
        out_specs=vmem,
        compiler_params=pltpu.CompilerParams(vmem_limit_bytes=VMEM_LIMIT),
    )(core, *arrays)


def lag_kernel(scale, table_ref, *refs):
    out = refs[-1]
    total = refs[0][...].astype(jnp.float32)
    for ref in refs[1:-1]:
        total += ref[...].astype(jnp.float32)
    cross = unpack(total)
    high = cross.astype(jnp.bfloat16)
    low = (cross - high.astype(jnp.float32)).astype(jnp.bfloat16)
    dot = functools.partial(jnp.dot, preferred_element_type=jnp.float32)
    top, bottom = table_ref[: 2 * LANES, :], table_ref[2 * LANES :, :]
    lags = dot(high, top) + (dot(low, top) + dot(high, bottom))
    out[...] = (scale * lags).reshape(out.shape)


def to_lags(scale, table, arrays):
    vmem = pl.BlockSpec(memory_space=pltpu.VMEM)
    return pl.pallas_call(
        functools.partial(lag_kernel, scale),
        out_shape=jax.ShapeDtypeStruct((4, BLOCK, LAGS), jnp.float32),
        in_specs=[vmem] * (1 + len(arrays)),
        out_specs=vmem,
        compiler_params=pltpu.CompilerParams(vmem_limit_bytes=VMEM_LIMIT),
    )(table, *arrays)


def from_peers(value, axis):
    size = lax.axis_size(axis)
    return [
        lax.ppermute(value, axis, [(i, (i + k) % size) for i in range(size)])
        for k in range(1, size)
    ]


def body(records, fir_taps, source_ids):
    samples = records.shape[2]
    chans, times, cores = (lax.axis_size(axis) for axis in ("chan", "tm", "rep"))
    me = lax.axis_index("chan").astype(jnp.int32).reshape(1)
    core = lax.axis_index("rep").astype(jnp.int32).reshape(1)
    cross = local_cross(me, source_ids, records, fir_taps.reshape(1, -1), jnp.asarray(dft_table(samples)))
    pieces = added([cross] + from_peers(cross, "rep"), chans)
    mesh = [(a, t, r) for a in range(chans) for t in range(times) for r in range(cores)]
    place = {where: index for index, where in enumerate(mesh)}
    arrived = []
    for turn in range(-(-times // cores)):
        for k in range(chans):
            pairs = []
            for a, t, r in mesh:
                ahead = turn * cores + r
                if ahead >= times or (ahead == 0 and k == 0):
                    continue
                pairs.append((place[a, t, r], place[(a + k) % chans, (t + ahead) % times, r]))
            arrived.append(lax.ppermute(pieces[k], ("chan", "tm", "rep"), pairs))
    total = gathered(core, [pieces[0]] + arrived)
    windows_all = records.shape[0] * chans * times * cores
    scale = 1.0 / math.sqrt(windows_all * BLOCK * BINS)
    return to_lags(scale, jnp.asarray(lag_table(samples)), [total] + from_peers(total, "rep"))


def solution(mesh):
    in_specs = (P(("chan", "tm", "rep"), "parts", None), P(), P("parts"))
    out_specs = P(None, ("parts", "chan"), None)
    return jax.shard_map(body, mesh=mesh, in_specs=in_specs, out_specs=out_specs, check_vma=False)
```

time: 1680 us -> 25 us (0.01)
  local copies, waits for them, and re-layouts: 1530 us -> 2.85 us
  waiting for transfers between devices: 120 us -> 7.69 us
    gather x2 -> x0, local copies, waits for them, and re-layouts: 1520 us -> none  [fir_matrix(): values = jnp.take(fir_taps, jnp.clip(offset, 0, taps - 1))]
    psum x2 -> x0, waiting for transfers between devices: 120 us -> none  [the longest x1 89 us: spread(): return lax.psum(kept, axis)]
  transfers between devices with their start and end apart: 3 -> 6, of which waited for: 2 -> 4; matrix products, arithmetic and copies ran while one was open for 91% -> 0% of each run, Pallas kernels for 0% -> 0%
where the time goes in v1:
time: 25 us; the launch traced here: 24.8 us
  starting transfers between devices  8.97 us (36%)
  waiting for transfers between devices  7.69 us (31%)
  Pallas kernels  5.26 us (21%)
  local copies, waits for them, and re-layouts  2.85 us (11%)
    ppermute x4, starting transfers between devices, body(): arrived.append(lax.ppermute(pieces[k], ('chan', 'tm', 'rep'), pairs))  7.58 us
    ppermute x4, waiting for transfers between devices, body(): arrived.append(lax.ppermute(pieces[k], ('chan', 'tm', 'rep'), pairs))  5.4 us
    pallas_call x1, Pallas kernels, local_cross(): pl.pallas_call(spectra_kernel, out_shape=jax.ShapeDtypeStruct((channels,...  4.09 us
    unnamed x10, local copies, waits for them, and re-layouts  2.85 us
    ppermute x2, waiting for transfers between devices, from_peers(): lax.ppermute(value, axis, [(i, (i + k) % size) for i in range(size)])  2.29 us
    ppermute x2, starting transfers between devices, from_peers(): lax.ppermute(value, axis, [(i, (i + k) % size) for i in range(size)])  1.4 us
    pallas_call x1, Pallas kernels, to_lags(): pl.pallas_call(functools.partial(lag_kernel, scale), out_shape=jax.ShapeD...  1 us
  transfers between devices with their start and end apart: 6, of which 4 were waited for; matrix products, arithmetic and copies ran while one was open for 0% of the time, Pallas kernels for 0%

profile of v1, /device:TPU:0, one launch (start us, length us, event | category | flops | bytes accessed | tf_op | source)
XLA Modules:
  0.0 24.8 jit_solution(18238937614604530874)
XLA Ops:
  0.0 0.0 copy-start.3
  0.0 0.0 copy-start.4
  0.0 0.7 %copy-done.3 = s32[4]{0:T(128)S(1)} copy-done((s32[4]{0:T(128)S(1)}, s32[4]{0:T(128)}, u32[]{:S(2)}) %copy-start.3) | copy-done | bytes 40
  0.7 0.0 copy-done.4
  0.7 0.0 copy-start
  0.7 1.2 %copy-done = bf16[4,256,512]{2,1,0:T(8,128)(2,1)S(1)} copy-done((bf16[4,256,512]{2,1,0:T(8,128)(2,1)S(1)}, bf16[4,256,512]{2,1,0:T(8,128)(2,1)}, u32[]{:S(2)}) %copy-start) | copy-done | bytes 1048600
  1.9 0.0 copy-start.2
  1.9 0.9 %copy-done.2 = bf16[512,256]{1,0:T(8,128)(2,1)S(1)} copy-done((bf16[512,256]{1,0:T(8,128)(2,1)S(1)}, bf16[512,256]{1,0:T(8,128)(2,1)}, u32[]{:S(2)}) %copy-start.2) | copy-done | bytes 262168
  2.8 4.1 %shard_map.55.refs_0_ = bf16[256,768]{1,0:T(8,128)(2,1)S(1)} custom-call(s32[1]{0:T(128)} %bitcast.1.me_ref, s32[4]{0:T(128)S(1)} %copy-done.3, bf16[4,256,512]{2,1,0:T(8,128)(2,1)S(1)} %copy-done, f32[1,65]{1,0:T(1,128)S(1)} %bitcast.3, bf16[512,256]{1,0:T(8,128)(2,1)S(1)} %copy-done.2), custom_call_target="tpu_custom_call" | custom-call | tf_op jit(solution)/shard_map/pallas_call | solution.py:133
  6.9 0.5 %collective-permute-start = (bf16[256,768]{1,0:T(8,128)(2,1)S(1)}, bf16[256,768]{1,0:T(8,128)(2,1)S(1)}, u32[]{:S(2)}, u32[]{:S(2)}) collective-permute-start(bf16[256,768]{1,0:T(8,128)(2,1)S(1)} %shard_map.55.refs_0_), channel_id=1, source_target_pairs={{0,1},{1,0},{2,3},{3,2},{4,5},{5,4},{6,7},{7,6},{8,9},{9,8},{10,11... | collective-permute-start | bytes 1179656 | tf_op jit(solution)/shard_map/ppermute | solution.py:219
  7.5 1.3 %collective-permute-done.refs_1_ = bf16[256,768]{1,0:T(8,128)(2,1)S(1)} collective-permute-done((bf16[256,768]{1,0:T(8,128)(2,1)S(1)}, bf16[256,768]{1,0:T(8,128)(2,1)S(1)}, u32[]{:S(2)}, u32[]{:S(2)}) %collective-permute-start) | collective-permute-done | bytes 393248 | tf_op jit(solution)/shard_map/ppermute | solution.py:219
  8.8 0.1 shard_map.56
  8.9 3.0 %collective-permute-start.2 = (bf16[64,768]{1,0:T(8,128)(2,1)S(1)}, bf16[64,768]{1,0:T(8,128)(2,1)S(1)}, u32[]{:S(2)}, u32[]{:S(2)}) collective-permute-start(bf16[64,768]{1,0:T(8,128)(2,1)S(1)} %get-tuple-element.10), channel_id=1, source_target_pairs={{0,4},{1,7},{2,6},{3,5},{4,8},{5,11},{6,10},{7,9},{8,12},{9,15},{1... | collective-permute-start | bytes 294920 | tf_op jit(solution)/shard_map/ppermute | solution.py:242
  11.9 2.6 %collective-permute-start.3 = (bf16[64,768]{1,0:T(8,128)(2,1)S(1)}, bf16[64,768]{1,0:T(8,128)(2,1)S(1)}, u32[]{:S(2)}, u32[]{:S(2)}) collective-permute-start(bf16[64,768]{1,0:T(8,128)(2,1)S(1)} %get-tuple-element.11), channel_id=1, source_target_pairs={{0,8},{1,11},{2,10},{3,9},{4,12},{5,15},{6,14},{7,13},{8,0},{9,3},... | collective-permute-start | bytes 294920 | tf_op jit(solution)/shard_map/ppermute | solution.py:242
  14.5 1.3 %collective-permute-start.4 = (bf16[64,768]{1,0:T(8,128)(2,1)S(1)}, bf16[64,768]{1,0:T(8,128)(2,1)S(1)}, u32[]{:S(2)}, u32[]{:S(2)}) collective-permute-start(bf16[64,768]{1,0:T(8,128)(2,1)S(1)} %get-tuple-element.12), channel_id=1, source_target_pairs={{0,12},{1,15},{2,14},{3,13},{4,0},{5,3},{6,2},{7,1},{8,4},{9,7},{1... | collective-permute-start | bytes 294920 | tf_op jit(solution)/shard_map/ppermute | solution.py:242
  15.9 0.7 %collective-permute-start.1 = (bf16[64,768]{1,0:T(8,128)(2,1)S(1)}, bf16[64,768]{1,0:T(8,128)(2,1)S(1)}, u32[]{:S(2)}, u32[]{:S(2)}) collective-permute-start(bf16[64,768]{1,0:T(8,128)(2,1)S(1)} %get-tuple-element.9.refs_0_), channel_id=1, source_target_pairs={{1,3},{3,1},{5,7},{7,5},{9,11},{11,9},{13,15},{15,13},{17,19},{19,... | collective-permute-start | bytes 294920 | tf_op jit(solution)/shard_map/ppermute | solution.py:242
  16.5 0.9 %collective-permute-done.2.refs_2_ = bf16[64,768]{1,0:T(8,128)(2,1)S(1)} collective-permute-done((bf16[64,768]{1,0:T(8,128)(2,1)S(1)}, bf16[64,768]{1,0:T(8,128)(2,1)S(1)}, u32[]{:S(2)}, u32[]{:S(2)}) %collective-permute-start.2) | collective-permute-done | bytes 98336 | tf_op jit(solution)/shard_map/ppermute | solution.py:242
  17.4 4.5 %collective-permute-done.3.refs_3_ = bf16[64,768]{1,0:T(8,128)(2,1)S(1)} collective-permute-done((bf16[64,768]{1,0:T(8,128)(2,1)S(1)}, bf16[64,768]{1,0:T(8,128)(2,1)S(1)}, u32[]{:S(2)}, u32[]{:S(2)}) %collective-permute-start.3) | collective-permute-done | bytes 98336 | tf_op jit(solution)/shard_map/ppermute | solution.py:242
  21.9 0.0 collective-permute-done.4.refs_4_
  21.9 0.0 collective-permute-done.1.refs_1_
  21.9 0.0 copy-start.1
  21.9 0.1 shard_map.57.refs_0_
  22.0 0.9 %collective-permute-start.5 = (bf16[64,768]{1,0:T(8,128)(2,1)S(1)}, bf16[64,768]{1,0:T(8,128)(2,1)S(1)}, u32[]{:S(2)}, u32[]{:S(2)}) collective-permute-start(bf16[64,768]{1,0:T(8,128)(2,1)S(1)} %shard_map.57.refs_0_), channel_id=1, source_target_pairs={{0,1},{1,0},{2,3},{3,2},{4,5},{5,4},{6,7},{7,6},{8,9},{9,8},{10,11... | collective-permute-start | bytes 294920 | tf_op jit(solution)/shard_map/ppermute | solution.py:219
  22.9 0.9 %collective-permute-done.5.refs_1_ = bf16[64,768]{1,0:T(8,128)(2,1)S(1)} collective-permute-done((bf16[64,768]{1,0:T(8,128)(2,1)S(1)}, bf16[64,768]{1,0:T(8,128)(2,1)S(1)}, u32[]{:S(2)}, u32[]{:S(2)}) %collective-permute-start.5) | collective-permute-done | bytes 98336 | tf_op jit(solution)/shard_map/ppermute | solution.py:219
  23.8 0.0 copy-done.1
  23.8 1.0 %shard_map.58 = f32[4,64,256]{2,1,0:T(8,128)} custom-call(bf16[512,256]{1,0:T(8,128)(2,1)S(1)} %copy-done.1, bf16[64,768]{1,0:T(8,128)(2,1)S(1)} %shard_map.57.refs_0_, bf16[64,768]{1,0:T(8,128)(2,1)S(1)} %collective-permute-done.5.refs_1_), custom_call_target="tpu_custom_call" | custom-call | tf_op jit(solution)/shard_map/pallas_call | solution.py:207
Async XLA Ops:
  0.0 0.7 %copy-start.3 = (s32[4]{0:T(128)S(1)}, s32[4]{0:T(128)}, u32[]{:S(2)}) copy-start(s32[4]{0:T(128)} %ids_ref.1) | copy-start | bytes 52
  0.0 0.7 %copy-start.4 = (f32[65]{0:T(128)S(1)}, f32[65]{0:T(128)}, u32[]{:S(2)}) copy-start(f32[65]{0:T(128)} %param.6) | copy-start | bytes 784
  0.7 1.2 %copy-start = (bf16[4,256,512]{2,1,0:T(8,128)(2,1)S(1)}, bf16[4,256,512]{2,1,0:T(8,128)(2,1)}, u32[]{:S(2)}) copy-start(bf16[4,256,512]{2,1,0:T(8,128)(2,1)} %rec_ref.1) | copy-start | bytes 3145732
  1.9 0.9 %copy-start.2 = (bf16[512,256]{1,0:T(8,128)(2,1)S(1)}, bf16[512,256]{1,0:T(8,128)(2,1)}, u32[]{:S(2)}) copy-start(bf16[512,256]{1,0:T(8,128)(2,1)} %constant.13.clone.dft_ref) | copy-start | bytes 786436
  6.9 1.9 %collective-permute-start = (bf16[256,768]{1,0:T(8,128)(2,1)S(1)}, bf16[256,768]{1,0:T(8,128)(2,1)S(1)}, u32[]{:S(2)}, u32[]{:S(2)}) collective-permute-start(bf16[256,768]{1,0:T(8,128)(2,1)S(1)} %shard_map.55.refs_0_), channel_id=1, source_target_pairs={{0,1},{1,0},{2,3},{3,2},{4,5},{5,4},{6,7},{7,6},{8,9},{9,8},{10,11... | collective-permute-start | bytes 1179656 | tf_op jit(solution)/shard_map/ppermute | solution.py:219
  8.9 8.5 %collective-permute-start.2 = (bf16[64,768]{1,0:T(8,128)(2,1)S(1)}, bf16[64,768]{1,0:T(8,128)(2,1)S(1)}, u32[]{:S(2)}, u32[]{:S(2)}) collective-permute-start(bf16[64,768]{1,0:T(8,128)(2,1)S(1)} %get-tuple-element.10), channel_id=1, source_target_pairs={{0,4},{1,7},{2,6},{3,5},{4,8},{5,11},{6,10},{7,9},{8,12},{9,15},{1... | collective-permute-start | bytes 294920 | tf_op jit(solution)/shard_map/ppermute | solution.py:242
  11.9 10.0 %collective-permute-start.3 = (bf16[64,768]{1,0:T(8,128)(2,1)S(1)}, bf16[64,768]{1,0:T(8,128)(2,1)S(1)}, u32[]{:S(2)}, u32[]{:S(2)}) collective-permute-start(bf16[64,768]{1,0:T(8,128)(2,1)S(1)} %get-tuple-element.11), channel_id=1, source_target_pairs={{0,8},{1,11},{2,10},{3,9},{4,12},{5,15},{6,14},{7,13},{8,0},{9,3},... | collective-permute-start | bytes 294920 | tf_op jit(solution)/shard_map/ppermute | solution.py:242
  14.5 7.4 %collective-permute-start.4 = (bf16[64,768]{1,0:T(8,128)(2,1)S(1)}, bf16[64,768]{1,0:T(8,128)(2,1)S(1)}, u32[]{:S(2)}, u32[]{:S(2)}) collective-permute-start(bf16[64,768]{1,0:T(8,128)(2,1)S(1)} %get-tuple-element.12), channel_id=1, source_target_pairs={{0,12},{1,15},{2,14},{3,13},{4,0},{5,3},{6,2},{7,1},{8,4},{9,7},{1... | collective-permute-start | bytes 294920 | tf_op jit(solution)/shard_map/ppermute | solution.py:242
  15.9 6.1 %collective-permute-start.1 = (bf16[64,768]{1,0:T(8,128)(2,1)S(1)}, bf16[64,768]{1,0:T(8,128)(2,1)S(1)}, u32[]{:S(2)}, u32[]{:S(2)}) collective-permute-start(bf16[64,768]{1,0:T(8,128)(2,1)S(1)} %get-tuple-element.9.refs_0_), channel_id=1, source_target_pairs={{1,3},{3,1},{5,7},{7,5},{9,11},{11,9},{13,15},{15,13},{17,19},{19,... | collective-permute-start | bytes 294920 | tf_op jit(solution)/shard_map/ppermute | solution.py:242
  21.9 1.9 %copy-start.1 = (bf16[512,256]{1,0:T(8,128)(2,1)S(1)}, bf16[512,256]{1,0:T(8,128)(2,1)}, u32[]{:S(2)}) copy-start(bf16[512,256]{1,0:T(8,128)(2,1)} %constant.14.clone.table_ref) | copy-start | bytes 786436
  22.0 1.8 %collective-permute-start.5 = (bf16[64,768]{1,0:T(8,128)(2,1)S(1)}, bf16[64,768]{1,0:T(8,128)(2,1)S(1)}, u32[]{:S(2)}, u32[]{:S(2)}) collective-permute-start(bf16[64,768]{1,0:T(8,128)(2,1)S(1)} %shard_map.57.refs_0_), channel_id=1, source_target_pairs={{0,1},{1,0},{2,3},{3,2},{4,5},{5,4},{6,7},{7,6},{8,9},{9,8},{10,11... | collective-permute-start | bytes 294920 | tf_op jit(solution)/shard_map/ppermute | solution.py:219

commit v2 on v1

--- a/solution.py
+++ b/solution.py
@@ -78,41 +78,84 @@
     return jnp.concatenate(rows + [jnp.concatenate(last, axis=1)], axis=0)
 
 
-def spectra_kernel(me_ref, ids_ref, rec_ref, taps_ref, dft_ref, out_ref, pad, fir, white, sums):
-    windows, channels, samples = rec_ref.shape
-    blocks = channels // BLOCK
+def spectra_kernel(
+    me_ref,
+    ids_hbm,
+    rec_hbm,
+    taps_hbm,
+    dft_hbm,
+    out_ref,
+    ids_ref,
+    rec_ref,
+    taps_ref,
+    dft_ref,
+    pad,
+    fir,
+    white,
+    sums,
+    small_sems,
+    dft_sem,
+    rec_sems,
+):
+    blocks, windows, width, samples = rec_ref.shape
     count = ids_ref.shape[0]
+    copies = [
+        pltpu.make_async_copy(taps_hbm, taps_ref, small_sems.at[0]),
+        pltpu.make_async_copy(ids_hbm, ids_ref, small_sems.at[1]),
+        pltpu.make_async_copy(dft_hbm, dft_ref, dft_sem),
+    ]
+    for copy in copies:
+        copy.start()
+    loads = [
+        pltpu.make_async_copy(
+            rec_hbm.at[:, pl.ds(width * b, width), :], rec_ref.at[b], rec_sems.at[b]
+        )
+        for b in range(blocks)
+    ]
+    for load in loads:
+        load.start()
+    fir[...] = jnp.zeros(fir.shape, fir.dtype)
+    rows = lax.broadcasted_iota(jnp.int32, (2 * LANES, 2 * LANES), 0) % LANES
+    cols = lax.broadcasted_iota(jnp.int32, (2 * LANES, 2 * LANES), 1)
+    near = (jnp.abs(rows - cols) <= 2) | (cols >= LANES)
+    gather = jnp.where(near, 1.0, 0.0).astype(jnp.bfloat16)
+    copies[0].wait()
     three = fir_blocks(taps_ref, pad).astype(jnp.bfloat16)
-    fir[...] = jnp.zeros(fir.shape, fir.dtype)
     tiles = samples // LANES
     for i in range(tiles):
         for j in range(max(i - 1, 0), min(i + 2, tiles)):
             fir[LANES * i : LANES * (i + 1), LANES * j : LANES * (j + 1)] = three[
                 :, LANES * (j - i + 1) : LANES * (j - i + 2)
             ]
+    copies[1].wait()
+    copies[2].wait()
     for b in range(blocks):
-        rows = rec_ref[:, BLOCK * b : BLOCK * (b + 1), :].reshape(windows * BLOCK, samples)
-        filtered = jnp.dot(rows, fir[...], preferred_element_type=jnp.float32).astype(jnp.bfloat16)
+        loads[b].wait()
+        block = rec_ref[b].reshape(windows * width, samples)
+        filtered = jnp.dot(block, fir[...], preferred_element_type=jnp.float32).astype(jnp.bfloat16)
         spectra = jnp.dot(filtered, dft_ref[...], preferred_element_type=jnp.float32)
         re, im = spectra[:, :LANES], spectra[:, LANES:]
         amp = jnp.sqrt(re * re + im * im)
-        pair = amp + pltpu.roll(amp, 1, 1)
-        smooth = (pltpu.roll(pair, LANES - 2, 1) + pair + pltpu.roll(amp, 2, 1)) / 5.0
-        mean_amp = jnp.sum(amp, axis=1, keepdims=True) / BINS + 1e-06
-        level = jnp.maximum(smooth, 0.5 * mean_amp)
-        scale = 1.0 / level
+        high = amp.astype(jnp.bfloat16)
+        low = (amp - high.astype(jnp.float32)).astype(jnp.bfloat16)
+        both = jnp.dot(
+            jnp.concatenate([high, low], axis=1), gather, preferred_element_type=jnp.float32
+        )
+        smooth = both[:, :LANES] * (1.0 / 5.0)
+        mean_amp = both[:, LANES:] * (1.0 / BINS) + 1e-06
+        scale = 1.0 / jnp.maximum(smooth, 0.5 * mean_amp)
         for which, value in enumerate((re, im)):
             unit = (value * scale).astype(jnp.bfloat16)
-            white[which, b] = unit.reshape(windows, BLOCK, LANES)
+            white[which, b] = unit.reshape(windows, width, LANES)
             sums[which, b] = jnp.sum(
-                unit.astype(jnp.float32).reshape(windows, BLOCK, LANES), axis=1
+                unit.astype(jnp.float32).reshape(windows, width, LANES), axis=1
             )
     for k in range(blocks):
-        b = lax.rem(me_ref[0] + k, blocks)
+        b = relative(me_ref[0], k, blocks)
         re, im = [], []
         for s in range(count):
-            total_re = jnp.zeros((BLOCK, LANES), jnp.float32)
-            total_im = jnp.zeros((BLOCK, LANES), jnp.float32)
+            total_re = jnp.zeros((width, LANES), jnp.float32)
+            total_im = jnp.zeros((width, LANES), jnp.float32)
             for w in range(windows):
                 src_re = sums[0, ids_ref[s], w : w + 1, :]
                 src_im = sums[1, ids_ref[s], w : w + 1, :]
@@ -122,27 +165,39 @@
                 total_im += white_im * src_re - white_re * src_im
             re.append(total_re)
             im.append(total_im)
-        out_ref[BLOCK * k : BLOCK * (k + 1), :] = pack(re, im).astype(jnp.bfloat16)
+        out_ref[width * k : width * (k + 1), :] = pack(re, im).astype(jnp.bfloat16)
+
+
+def relative(me, k, size):
+    if size & (size - 1) == 0:
+        return me ^ k
+    return (me + k) % size
 
 
 def local_cross(me, source_ids, records, taps, dft):
     windows, channels, samples = records.shape
     blocks = channels // BLOCK
-    vmem = pl.BlockSpec(memory_space=pltpu.VMEM)
-    smem = pl.BlockSpec(memory_space=pltpu.SMEM)
+    hbm = pl.BlockSpec(memory_space=pltpu.HBM)
     return pl.pallas_call(
         spectra_kernel,
         out_shape=jax.ShapeDtypeStruct((channels, 6 * LANES), jnp.bfloat16),
-        in_specs=[smem, smem, vmem, vmem, vmem],
-        out_specs=vmem,
+        in_specs=[pl.BlockSpec(memory_space=pltpu.SMEM), hbm, hbm, hbm, hbm],
+        out_specs=pl.BlockSpec(memory_space=pltpu.VMEM),
         scratch_shapes=[
+            pltpu.SMEM(source_ids.shape, jnp.int32),
+            pltpu.VMEM((blocks, windows, BLOCK, samples), jnp.bfloat16),
+            pltpu.VMEM(taps.shape, jnp.float32),
+            pltpu.VMEM(dft.shape, jnp.bfloat16),
             pltpu.VMEM((8, LANES), jnp.float32),
             pltpu.VMEM((samples, samples), jnp.bfloat16),
             pltpu.VMEM((2, blocks, windows, BLOCK, LANES), jnp.bfloat16),
             pltpu.VMEM((2, blocks, windows, LANES), jnp.float32),
+            pltpu.SemaphoreType.DMA((2,)),
+            pltpu.SemaphoreType.DMA,
+            pltpu.SemaphoreType.DMA((blocks,)),
         ],
         compiler_params=pltpu.CompilerParams(vmem_limit_bytes=VMEM_LIMIT),
-    )(me, source_ids, records, taps, dft)
+    )(me, *(pltpu.with_memory_space_constraint(v, pltpu.HBM) for v in (source_ids, records, taps, dft)))
 
 
 def add_kernel(pieces, *refs):
@@ -238,7 +293,7 @@
                 ahead = turn * cores + r
                 if ahead >= times or (ahead == 0 and k == 0):
                     continue
-                pairs.append((place[a, t, r], place[(a + k) % chans, (t + ahead) % times, r]))
+                pairs.append((place[a, t, r], place[relative(a, k, chans), (t + ahead) % times, r]))
             arrived.append(lax.ppermute(pieces[k], ("chan", "tm", "rep"), pairs))
     total = gathered(core, [pieces[0]] + arrived)
     windows_all = records.shape[0] * chans * times * cores

time: 25 us -> 23 us (0.920)
  local copies, waits for them, and re-layouts: 2.85 us -> 0.01 us
  waiting for transfers between devices: 7.69 us -> 9.67 us
  starting transfers between devices: 8.97 us -> 7.32 us
  Pallas kernels: 5.26 us -> 5.66 us
    unnamed x10 -> x2, local copies, waits for them, and re-layouts: 2.85 us -> 0.01 us
    ppermute x4, waiting for transfers between devices: 5.4 us -> 7.38 us  [body(): arrived.append(lax.ppermute(pieces[k], ('chan', 'tm', 'rep'), pairs))]
    ppermute x4, starting transfers between devices: 7.58 us -> 6.25 us  [body(): arrived.append(lax.ppermute(pieces[k], ('chan', 'tm', 'rep'), pairs))]
    pallas_call x1, Pallas kernels: 4.09 us -> 4.49 us  [local_cross(): pl.pallas_call(spectra_kernel, out_shape=jax.ShapeDtypeStruct((channels,...]
    ppermute x2, starting transfers between devices: 1.4 us -> 1.07 us  [from_peers(): lax.ppermute(value, axis, [(i, (i + k) % size) for i in range(size)])]
  transfers between devices with their start and end apart: 6 -> 6, of which waited for: 4 -> 3; matrix products, arithmetic and copies ran while one was open for 0% -> 0% of each run, Pallas kernels for 0% -> 0%
where the time goes in v2:
time: 23 us; the launch traced here: 22.7 us
  waiting for transfers between devices  9.67 us (42%)
  starting transfers between devices  7.32 us (32%)
  Pallas kernels  5.66 us (25%)
    ppermute x4, waiting for transfers between devices, body(): arrived.append(lax.ppermute(pieces[k], ('chan', 'tm', 'rep'), pairs))  7.38 us
    ppermute x4, starting transfers between devices, body(): arrived.append(lax.ppermute(pieces[k], ('chan', 'tm', 'rep'), pairs))  6.25 us
    pallas_call x1, Pallas kernels, local_cross(): pl.pallas_call(spectra_kernel, out_shape=jax.ShapeDtypeStruct((channels,...  4.49 us
    ppermute x2, waiting for transfers between devices, from_peers(): lax.ppermute(value, axis, [(i, (i + k) % size) for i in range(size)])  2.29 us
    ppermute x2, starting transfers between devices, from_peers(): lax.ppermute(value, axis, [(i, (i + k) % size) for i in range(size)])  1.07 us
    pallas_call x1, Pallas kernels, to_lags(): pl.pallas_call(functools.partial(lag_kernel, scale), out_shape=jax.ShapeD...  1 us
  transfers between devices with their start and end apart: 6, of which 3 were waited for; matrix products, arithmetic and copies ran while one was open for 0% of the time, Pallas kernels for 0%

profile of v2, /device:TPU:0, one launch (start us, length us, event | category | flops | bytes accessed | tf_op | source)
XLA Modules:
  0.0 22.7 jit_solution(18156053279274545607)
XLA Ops:
  0.0 4.5 %shard_map.55.refs_0_ = bf16[256,768]{1,0:T(8,128)(2,1)S(1)} custom-call(s32[1]{0:T(128)} %bitcast.1.me_ref, s32[4]{0:T(128)} %ids_hbm.1, bf16[4,256,512]{2,1,0:T(8,128)(2,1)} %rec_hbm.1, f32[1,65]{1,0:T(1,128)} %bitcast.3, bf16[512,256]{1,0:T(8,128)(2,1)} %constant.13.clone.dft_hbm), custom_call_target="tpu_custom_call" | custom-call | tf_op jit(solution)/shard_map/pallas_call | solution.py:181
  4.5 0.5 %collective-permute-start = (bf16[256,768]{1,0:T(8,128)(2,1)S(1)}, bf16[256,768]{1,0:T(8,128)(2,1)S(1)}, u32[]{:S(2)}, u32[]{:S(2)}) collective-permute-start(bf16[256,768]{1,0:T(8,128)(2,1)S(1)} %shard_map.55.refs_0_), channel_id=1, source_target_pairs={{0,1},{1,0},{2,3},{3,2},{4,5},{5,4},{6,7},{7,6},{8,9},{9,8},{10,11... | collective-permute-start | bytes 1179656 | tf_op jit(solution)/shard_map/ppermute | solution.py:274
  5.0 1.3 %collective-permute-done.refs_1_ = bf16[256,768]{1,0:T(8,128)(2,1)S(1)} collective-permute-done((bf16[256,768]{1,0:T(8,128)(2,1)S(1)}, bf16[256,768]{1,0:T(8,128)(2,1)S(1)}, u32[]{:S(2)}, u32[]{:S(2)}) %collective-permute-start) | collective-permute-done | bytes 393248 | tf_op jit(solution)/shard_map/ppermute | solution.py:274
  6.4 0.1 shard_map.56
  6.5 3.0 %collective-permute-start.2 = (bf16[64,768]{1,0:T(8,128)(2,1)S(1)}, bf16[64,768]{1,0:T(8,128)(2,1)S(1)}, u32[]{:S(2)}, u32[]{:S(2)}) collective-permute-start(bf16[64,768]{1,0:T(8,128)(2,1)S(1)} %get-tuple-element.10), channel_id=1, source_target_pairs={{0,4},{1,7},{2,6},{3,5},{4,0},{5,3},{6,2},{7,1},{8,12},{9,15},{10,... | collective-permute-start | bytes 294920 | tf_op jit(solution)/shard_map/ppermute | solution.py:297
  9.5 2.6 %collective-permute-start.3 = (bf16[64,768]{1,0:T(8,128)(2,1)S(1)}, bf16[64,768]{1,0:T(8,128)(2,1)S(1)}, u32[]{:S(2)}, u32[]{:S(2)}) collective-permute-start(bf16[64,768]{1,0:T(8,128)(2,1)S(1)} %get-tuple-element.11), channel_id=1, source_target_pairs={{0,8},{1,11},{2,10},{3,9},{4,12},{5,15},{6,14},{7,13},{8,0},{9,3},... | collective-permute-start | bytes 294920 | tf_op jit(solution)/shard_map/ppermute | solution.py:297
  12.1 0.0 collective-permute-start.4
  12.1 0.7 %collective-permute-start.1 = (bf16[64,768]{1,0:T(8,128)(2,1)S(1)}, bf16[64,768]{1,0:T(8,128)(2,1)S(1)}, u32[]{:S(2)}, u32[]{:S(2)}) collective-permute-start(bf16[64,768]{1,0:T(8,128)(2,1)S(1)} %get-tuple-element.9.refs_0_), channel_id=1, source_target_pairs={{1,3},{3,1},{5,7},{7,5},{9,11},{11,9},{13,15},{15,13},{17,19},{19,... | collective-permute-start | bytes 294920 | tf_op jit(solution)/shard_map/ppermute | solution.py:297
  12.7 0.0 collective-permute-done.2.refs_2_
  12.7 7.4 %collective-permute-done.3.refs_3_ = bf16[64,768]{1,0:T(8,128)(2,1)S(1)} collective-permute-done((bf16[64,768]{1,0:T(8,128)(2,1)S(1)}, bf16[64,768]{1,0:T(8,128)(2,1)S(1)}, u32[]{:S(2)}, u32[]{:S(2)}) %collective-permute-start.3) | collective-permute-done | bytes 98336 | tf_op jit(solution)/shard_map/ppermute | solution.py:297
  20.1 0.0 collective-permute-done.4.refs_4_
  20.1 0.0 collective-permute-done.1.refs_1_
  20.1 0.0 copy-start
  20.1 0.1 shard_map.57.refs_0_
  20.2 0.5 %collective-permute-start.5 = (bf16[64,768]{1,0:T(8,128)(2,1)S(1)}, bf16[64,768]{1,0:T(8,128)(2,1)S(1)}, u32[]{:S(2)}, u32[]{:S(2)}) collective-permute-start(bf16[64,768]{1,0:T(8,128)(2,1)S(1)} %shard_map.57.refs_0_), channel_id=1, source_target_pairs={{0,1},{1,0},{2,3},{3,2},{4,5},{5,4},{6,7},{7,6},{8,9},{9,8},{10,11... | collective-permute-start | bytes 294920 | tf_op jit(solution)/shard_map/ppermute | solution.py:274
  20.8 0.9 %collective-permute-done.5.refs_1_ = bf16[64,768]{1,0:T(8,128)(2,1)S(1)} collective-permute-done((bf16[64,768]{1,0:T(8,128)(2,1)S(1)}, bf16[64,768]{1,0:T(8,128)(2,1)S(1)}, u32[]{:S(2)}, u32[]{:S(2)}) %collective-permute-start.5) | collective-permute-done | bytes 98336 | tf_op jit(solution)/shard_map/ppermute | solution.py:274
  21.7 0.0 copy-done
  21.7 1.0 %shard_map.58 = f32[4,64,256]{2,1,0:T(8,128)} custom-call(bf16[512,256]{1,0:T(8,128)(2,1)S(1)} %copy-done, bf16[64,768]{1,0:T(8,128)(2,1)S(1)} %shard_map.57.refs_0_, bf16[64,768]{1,0:T(8,128)(2,1)S(1)} %collective-permute-done.5.refs_1_), custom_call_target="tpu_custom_call" | custom-call | tf_op jit(solution)/shard_map/pallas_call | solution.py:262
Async XLA Ops:
  4.5 1.9 %collective-permute-start = (bf16[256,768]{1,0:T(8,128)(2,1)S(1)}, bf16[256,768]{1,0:T(8,128)(2,1)S(1)}, u32[]{:S(2)}, u32[]{:S(2)}) collective-permute-start(bf16[256,768]{1,0:T(8,128)(2,1)S(1)} %shard_map.55.refs_0_), channel_id=1, source_target_pairs={{0,1},{1,0},{2,3},{3,2},{4,5},{5,4},{6,7},{7,6},{8,9},{9,8},{10,11... | collective-permute-start | bytes 1179656 | tf_op jit(solution)/shard_map/ppermute | solution.py:274
  6.5 6.3 %collective-permute-start.2 = (bf16[64,768]{1,0:T(8,128)(2,1)S(1)}, bf16[64,768]{1,0:T(8,128)(2,1)S(1)}, u32[]{:S(2)}, u32[]{:S(2)}) collective-permute-start(bf16[64,768]{1,0:T(8,128)(2,1)S(1)} %get-tuple-element.10), channel_id=1, source_target_pairs={{0,4},{1,7},{2,6},{3,5},{4,0},{5,3},{6,2},{7,1},{8,12},{9,15},{10,... | collective-permute-start | bytes 294920 | tf_op jit(solution)/shard_map/ppermute | solution.py:297
  9.5 10.6 %collective-permute-start.3 = (bf16[64,768]{1,0:T(8,128)(2,1)S(1)}, bf16[64,768]{1,0:T(8,128)(2,1)S(1)}, u32[]{:S(2)}, u32[]{:S(2)}) collective-permute-start(bf16[64,768]{1,0:T(8,128)(2,1)S(1)} %get-tuple-element.11), channel_id=1, source_target_pairs={{0,8},{1,11},{2,10},{3,9},{4,12},{5,15},{6,14},{7,13},{8,0},{9,3},... | collective-permute-start | bytes 294920 | tf_op jit(solution)/shard_map/ppermute | solution.py:297
  12.1 8.1 %collective-permute-start.4 = (bf16[64,768]{1,0:T(8,128)(2,1)S(1)}, bf16[64,768]{1,0:T(8,128)(2,1)S(1)}, u32[]{:S(2)}, u32[]{:S(2)}) collective-permute-start(bf16[64,768]{1,0:T(8,128)(2,1)S(1)} %get-tuple-element.12), channel_id=1, source_target_pairs={{0,12},{1,15},{2,14},{3,13},{4,8},{5,11},{6,10},{7,9},{8,4},{9,7},... | collective-permute-start | bytes 294920 | tf_op jit(solution)/shard_map/ppermute | solution.py:297
  12.1 8.1 %collective-permute-start.1 = (bf16[64,768]{1,0:T(8,128)(2,1)S(1)}, bf16[64,768]{1,0:T(8,128)(2,1)S(1)}, u32[]{:S(2)}, u32[]{:S(2)}) collective-permute-start(bf16[64,768]{1,0:T(8,128)(2,1)S(1)} %get-tuple-element.9.refs_0_), channel_id=1, source_target_pairs={{1,3},{3,1},{5,7},{7,5},{9,11},{11,9},{13,15},{15,13},{17,19},{19,... | collective-permute-start | bytes 294920 | tf_op jit(solution)/shard_map/ppermute | solution.py:297
  20.1 1.6 %copy-start = (bf16[512,256]{1,0:T(8,128)(2,1)S(1)}, bf16[512,256]{1,0:T(8,128)(2,1)}, u32[]{:S(2)}) copy-start(bf16[512,256]{1,0:T(8,128)(2,1)} %constant.14.clone.table_ref) | copy-start | bytes 786436
  20.2 1.5 %collective-permute-start.5 = (bf16[64,768]{1,0:T(8,128)(2,1)S(1)}, bf16[64,768]{1,0:T(8,128)(2,1)S(1)}, u32[]{:S(2)}, u32[]{:S(2)}) collective-permute-start(bf16[64,768]{1,0:T(8,128)(2,1)S(1)} %shard_map.57.refs_0_), channel_id=1, source_target_pairs={{0,1},{1,0},{2,3},{3,2},{4,5},{5,4},{6,7},{7,6},{8,9},{9,8},{10,11... | collective-permute-start | bytes 294920 | tf_op jit(solution)/shard_map/ppermute | solution.py:274

commit v3 on v2

v3 whole, which is shorter than its diff:
```python
import functools
import math

import jax
import jax.numpy as jnp
import numpy as np
from jax import lax
from jax.experimental import pallas as pl
from jax.experimental.pallas import tpu as pltpu
from jax.sharding import PartitionSpec as P

BINS = 96
LAGS = 256
BLOCK = 64
LANES = 128
VMEM_LIMIT = 32 * 1024 * 1024


def dft_table(samples):
    times = np.arange(samples)[:, None]
    freqs = np.arange(1, BINS + 1)[None, :]
    angle = np.float32(2.0 * math.pi / samples) * (times * freqs % samples).astype(np.float32)
    table = np.zeros((samples, 2 * LANES), np.float32)
    table[:, :BINS] = np.cos(angle)
    table[:, LANES : LANES + BINS] = -np.sin(angle)
    return table.astype(jnp.bfloat16)


def lag_table(samples):
    freqs = np.arange(1, BINS + 1)[:, None]
    shifts = np.arange(LAGS)[None, :] - LAGS // 2
    angle = np.float32(2.0 * math.pi / samples) * np.mod(freqs * shifts, samples).astype(np.float32)
    table = np.zeros((2 * LANES, LAGS), np.float32)
    table[:BINS] = np.cos(angle)
    table[LANES : LANES + BINS] = -np.sin(angle)
    high = table.astype(jnp.bfloat16)
    low = (table - high.astype(np.float32)).astype(jnp.bfloat16)
    return np.concatenate([high, low], axis=0)


def fir_blocks(taps_ref, pad_ref):
    taps = taps_ref.shape[1]
    half = taps // 2
    pad_ref[...] = jnp.zeros(pad_ref.shape, jnp.float32)
    pad_ref[0:1, 0:taps] = taps_ref[...]
    rows = lax.broadcasted_iota(jnp.int32, (LANES, LANES), 0)
    cols = lax.broadcasted_iota(jnp.int32, (LANES, LANES), 1)
    flip = (rows + cols == taps - 1).astype(jnp.bfloat16)
    turned = jnp.dot(
        pad_ref[...].astype(jnp.bfloat16), flip, preferred_element_type=jnp.float32
    )[0:1]
    wide = jnp.concatenate([turned, jnp.zeros((1, 2 * LANES), jnp.float32)], axis=1)
    wide = jnp.broadcast_to(wide, (LANES, 3 * LANES))
    return pltpu.roll(wide, LANES - half, 1, stride=1, stride_axis=0)


def pack(re, im):
    lane = lax.broadcasted_iota(jnp.int32, re[0].shape, 1)
    tiles = []
    for index in range(3):
        for part, last in ((re[index], re[3]), (im[index], im[3])):
            moved = pltpu.roll(last, BINS - 32 * index, 1)
            tiles.append(jnp.where(lane < BINS, part, moved))
    return jnp.concatenate(tiles, axis=1)


def unpack(packed):
    lane = lax.broadcasted_iota(jnp.int32, (packed.shape[0], LANES), 1)
    tiles = [packed[:, LANES * i : LANES * (i + 1)] for i in range(6)]
    last = []
    for which in range(2):
        total = jnp.zeros_like(tiles[0])
        for index in range(3):
            moved = pltpu.roll(tiles[2 * index + which], LANES - BINS + 32 * index, 1)
            total = jnp.where((lane >= 32 * index) & (lane < 32 * index + 32), moved, total)
        last.append(total)
    rows = [jnp.concatenate([tiles[2 * i], tiles[2 * i + 1]], axis=1) for i in range(3)]
    return jnp.concatenate(rows + [jnp.concatenate(last, axis=1)], axis=0)


def spectra_kernel(
    place_ref,
    ids_hbm,
    rec_hbm,
    taps_hbm,
    dft_hbm,
    out_ref,
    kept_ref,
    ids_ref,
    rec_ref,
    taps_ref,
    dft_ref,
    pad,
    fir,
    white,
    sums,
    small_sems,
    dft_sem,
    rec_sems,
):
    blocks, windows, width, samples = rec_ref.shape
    count = ids_ref.shape[0]
    copies = [
        pltpu.make_async_copy(taps_hbm, taps_ref, small_sems.at[0]),
        pltpu.make_async_copy(ids_hbm, ids_ref, small_sems.at[1]),
        pltpu.make_async_copy(dft_hbm, dft_ref, dft_sem),
    ]
    for copy in copies:
        copy.start()
    loads = [
        pltpu.make_async_copy(
            rec_hbm.at[:, pl.ds(width * b, width), :], rec_ref.at[b], rec_sems.at[b]
        )
        for b in range(blocks)
    ]
    for load in loads:
        load.start()
    fir[...] = jnp.zeros(fir.shape, fir.dtype)
    rows = lax.broadcasted_iota(jnp.int32, (2 * LANES, 2 * LANES), 0) % LANES
    cols = lax.broadcasted_iota(jnp.int32, (2 * LANES, 2 * LANES), 1)
    near = (jnp.abs(rows - cols) <= 2) | (cols >= LANES)
    gather = jnp.where(near, 1.0, 0.0).astype(jnp.bfloat16)
    copies[0].wait()
    three = fir_blocks(taps_ref, pad).astype(jnp.bfloat16)
    tiles = samples // LANES
    for i in range(tiles):
        for j in range(max(i - 1, 0), min(i + 2, tiles)):
            fir[LANES * i : LANES * (i + 1), LANES * j : LANES * (j + 1)] = three[
                :, LANES * (j - i + 1) : LANES * (j - i + 2)
            ]
    copies[2].wait()
    both_tables = jnp.dot(fir[...], dft_ref[...], preferred_element_type=jnp.float32).astype(
        jnp.bfloat16
    )
    copies[1].wait()
    for load in loads:
        load.wait()
    spectra, both = [], []
    for b in range(blocks):
        block = rec_ref[b].reshape(windows * width, samples)
        spectra.append(jnp.dot(block, both_tables, preferred_element_type=jnp.float32))
    for b in range(blocks):
        re, im = spectra[b][:, :LANES], spectra[b][:, LANES:]
        amp = jnp.sqrt(re * re + im * im)
        high = amp.astype(jnp.bfloat16)
        low = (amp - high.astype(jnp.float32)).astype(jnp.bfloat16)
        both.append(
            jnp.dot(
                jnp.concatenate([high, low], axis=1), gather, preferred_element_type=jnp.float32
            )
        )
    for b in range(blocks):
        smooth = both[b][:, :LANES] * (1.0 / 5.0)
        mean_amp = both[b][:, LANES:] * (1.0 / BINS) + 1e-06
        scale = 1.0 / jnp.maximum(smooth, 0.5 * mean_amp)
        for which in range(2):
            value = spectra[b][:, LANES * which : LANES * (which + 1)]
            unit = (value * scale).astype(jnp.bfloat16)
            white[which, b] = unit.reshape(windows, width, LANES)
            sums[which, b] = jnp.sum(
                unit.astype(jnp.float32).reshape(windows, width, LANES), axis=1
            )

    def cross(k, rows):
        b = relative(place_ref[0], k, blocks)
        re, im = [], []
        for s in range(count):
            total_re = jnp.zeros((rows.size, LANES), jnp.float32)
            total_im = jnp.zeros((rows.size, LANES), jnp.float32)
            for w in range(windows):
                src_re = sums[0, ids_ref[s], w : w + 1, :]
                src_im = sums[1, ids_ref[s], w : w + 1, :]
                white_re = white[0, b, w, rows, :].astype(jnp.float32)
                white_im = white[1, b, w, rows, :].astype(jnp.float32)
                total_re += white_re * src_re + white_im * src_im
                total_im += white_im * src_re - white_re * src_im
            re.append(total_re)
            im.append(total_im)
        return pack(re, im).astype(jnp.bfloat16)

    whole, shared = kinds(blocks)
    half = width // 2
    mine = pl.ds(pl.multiple_of(place_ref[1] * half, half), half)
    theirs = pl.ds(pl.multiple_of((1 - place_ref[1]) * half, half), half)
    for i, k in enumerate(whole):
        out_ref[width * i : width * (i + 1), :] = cross(k, pl.ds(0, width))
    for i, k in enumerate(shared):
        start = width * len(whole) + half * i
        out_ref[start : start + half, :] = cross(k, theirs)
        kept_ref[half * i : half * (i + 1), :] = cross(k, mine)


def kinds(blocks):
    return list(range(3 * blocks // 4 - 1, 0, -1)), list(range(3 * blocks // 4, blocks)) + [0]


def relative(me, k, size):
    if size & (size - 1) == 0:
        return me ^ k
    return (me + k) % size


def local_cross(place, source_ids, records, taps, dft):
    windows, channels, samples = records.shape
    blocks = channels // BLOCK
    whole, shared = (len(kind) for kind in kinds(blocks))
    half = BLOCK // 2
    hbm = pl.BlockSpec(memory_space=pltpu.HBM)
    return pl.pallas_call(
        spectra_kernel,
        out_shape=[
            jax.ShapeDtypeStruct((BLOCK * whole + half * shared, 6 * LANES), jnp.bfloat16),
            jax.ShapeDtypeStruct((half * shared, 6 * LANES), jnp.bfloat16),
        ],
        in_specs=[pl.BlockSpec(memory_space=pltpu.SMEM), hbm, hbm, hbm, hbm],
        out_specs=[pl.BlockSpec(memory_space=pltpu.VMEM)] * 2,
        scratch_shapes=[
            pltpu.SMEM(source_ids.shape, jnp.int32),
            pltpu.VMEM((blocks, windows, BLOCK, samples), jnp.bfloat16),
            pltpu.VMEM(taps.shape, jnp.float32),
            pltpu.VMEM(dft.shape, jnp.bfloat16),
            pltpu.VMEM((8, LANES), jnp.float32),
            pltpu.VMEM((samples, samples), jnp.bfloat16),
            pltpu.VMEM((2, blocks, windows, BLOCK, LANES), jnp.bfloat16),
            pltpu.VMEM((2, blocks, windows, LANES), jnp.float32),
            pltpu.SemaphoreType.DMA((2,)),
            pltpu.SemaphoreType.DMA,
            pltpu.SemaphoreType.DMA((blocks,)),
        ],
        compiler_params=pltpu.CompilerParams(vmem_limit_bytes=VMEM_LIMIT),
    )(place, *(pltpu.with_memory_space_constraint(v, pltpu.HBM) for v in (source_ids, records, taps, dft)))


def tree(values):
    while len(values) > 1:
        values = [sum(values[i + 1 : i + 2], values[i]) for i in range(0, len(values), 2)]
    return values[0]


def add_kernel(whole, own, kept, other, *outs):
    rows = outs[0].shape[0]
    for i, out in enumerate(outs):
        if i < whole:
            at = slice(rows * i, rows * (i + 1))
            mine = own[at, :]
        else:
            half = out.shape[0]
            mine = kept[half * (i - whole) : half * (i - whole + 1), :]
            start = rows * whole + half * (i - whole)
            at = slice(start, start + half)
        total = mine.astype(jnp.float32) + other[at, :].astype(jnp.float32)
        out[...] = total.astype(out.dtype)


def tree_kernel(*refs):
    refs[-1][...] = tree([ref[...].astype(jnp.float32) for ref in refs[:-1]]).astype(refs[-1].dtype)


def core_kernel(turns, shares, *refs):
    out = refs[-1]
    arrived = [ref[...].astype(jnp.float32) for ref in refs[:-1]]
    share, arrived = tree(arrived[:shares]), arrived[shares:]
    blocks = [tree(arrived[i : i + turns]) for i in range(0, len(arrived), turns)]
    total = functools.reduce(jnp.add, blocks)
    rows = total.shape[0]
    out[:rows, :] = total.astype(out.dtype)
    out[rows:, :] = share.astype(out.dtype)


def lag_kernel(scale, place_ref, table_ref, own, other, out, total):
    rows = total.shape[0]
    half = rows // 2
    total[...] = own[:rows, :].astype(jnp.float32) + other[:rows, :].astype(jnp.float32)
    for core, ref in ((place_ref[1], own), (1 - place_ref[1], other)):
        at = pl.ds(pl.multiple_of(core * half, half), half)
        total[at, :] += ref[rows:, :].astype(jnp.float32)
    cross = unpack(total[...])
    high = cross.astype(jnp.bfloat16)
    low = (cross - high.astype(jnp.float32)).astype(jnp.bfloat16)
    dot = functools.partial(jnp.dot, preferred_element_type=jnp.float32)
    top, bottom = table_ref[: 2 * LANES, :], table_ref[2 * LANES :, :]
    lags = dot(high, top) + (dot(low, top) + dot(high, bottom))
    out[...] = (scale * lags).reshape(out.shape)


def in_vmem(kernel, out_shape, inputs, scalars=0, scratch=()):
    vmem = pl.BlockSpec(memory_space=pltpu.VMEM)
    smem = pl.BlockSpec(memory_space=pltpu.SMEM)
    several = isinstance(out_shape, list)
    return pl.pallas_call(
        kernel,
        out_shape=out_shape,
        in_specs=[smem] * scalars + [vmem] * (len(inputs) - scalars),
        out_specs=[vmem] * len(out_shape) if several else vmem,
        scratch_shapes=scratch,
        compiler_params=pltpu.CompilerParams(vmem_limit_bytes=VMEM_LIMIT),
    )(*inputs)


def body(records, fir_taps, source_ids):
    samples = records.shape[2]
    chans, times, cores = (lax.axis_size(axis) for axis in ("chan", "tm", "rep"))
    assert cores == 2
    axes = ("chan", "tm", "rep")
    devices = [(a, t, r) for a in range(chans) for t in range(times) for r in range(cores)]
    number = {device: i for i, device in enumerate(devices)}

    def send(value, to):
        return lax.ppermute(value, axes, [(number[d], number[to(*d)]) for d in devices])

    place = jnp.stack([lax.axis_index("chan"), lax.axis_index("rep")]).astype(jnp.int32)
    own, kept = local_cross(
        place, source_ids, records, fir_taps.reshape(1, -1), jnp.asarray(dft_table(samples))
    )
    width, half = 6 * LANES, BLOCK // 2
    whole, shared = kinds(chans)
    other = send(own, lambda a, t, r: (a, t, 1 - r))
    full = jax.ShapeDtypeStruct((BLOCK, width), jnp.bfloat16)
    part = jax.ShapeDtypeStruct((half, width), jnp.bfloat16)
    pieces = in_vmem(
        functools.partial(add_kernel, len(whole)),
        [full] * len(whole) + [part] * len(shared),
        [own, kept, other],
    )
    shares = [
        send(piece, lambda a, t, r, k=k: (relative(a, k, chans), t, r))
        for k, piece in zip(shared[:-1], pieces[len(whole) :])
    ]
    arrived = [
        send(piece, lambda a, t, r, k=k: (relative(a, k, chans), relative(t, turn + r, times), r))
        for k, piece in zip(whole, pieces)
        for turn in range(0, times, cores)
    ]
    share = in_vmem(tree_kernel, part, [pieces[-1]] + shares)
    shares = [share] + [
        send(share, lambda a, t, r, j=j: (a, relative(t, j, times), r)) for j in range(1, times)
    ]
    total = in_vmem(
        functools.partial(core_kernel, -(-times // cores), times),
        jax.ShapeDtypeStruct((BLOCK + half, width), jnp.bfloat16),
        shares + arrived,
    )
    other = send(total, lambda a, t, r: (a, t, 1 - r))
    windows_all = records.shape[0] * chans * times * cores
    scale = 1.0 / math.sqrt(windows_all * BLOCK * BINS)
    return in_vmem(
        functools.partial(lag_kernel, scale),
        jax.ShapeDtypeStruct((source_ids.shape[0], BLOCK, LAGS), jnp.float32),
        [place, jnp.asarray(lag_table(samples)), total, other],
        scalars=1,
        scratch=[pltpu.VMEM((BLOCK, width), jnp.float32)],
    )


def solution(mesh):
    in_specs = (P(("chan", "tm", "rep"), "parts", None), P(), P("parts"))
    out_specs = P(None, ("parts", "chan"), None)
    return jax.shard_map(body, mesh=mesh, in_specs=in_specs, out_specs=out_specs, check_vma=False)
```

time: 23 us -> 21.4 us (0.930)
  waiting for transfers between devices: 9.67 us -> 7.75 us
  starting transfers between devices: 7.32 us -> 8.02 us
  Pallas kernels: 5.66 us -> 5.36 us
    ppermute x6, waiting for transfers between devices: 9.67 us -> 7.75 us  [send(): lax.ppermute(value, axes, [(number[d], number[to(*d)]) for d in devices])]
    ppermute x6, starting transfers between devices: 7.32 us -> 8.02 us  [send(): lax.ppermute(value, axes, [(number[d], number[to(*d)]) for d in devices])]
    pallas_call x4 -> x5, Pallas kernels: 5.66 us -> 5.36 us  [the longest x1 3.65 us: local_cross(): pl.pallas_call(spectra_kernel, out_shape=[jax.ShapeDtypeStruct((BLOCK * w...]
  transfers between devices with their start and end apart: 6 -> 6, of which waited for: 3 -> 5; matrix products, arithmetic and copies ran while one was open for 0% -> 0% of each run, Pallas kernels for 0% -> 0%
where the time goes in v3:
time: 21.4 us; the launch traced here: 21.2 us
  starting transfers between devices  8.02 us (37%)
  waiting for transfers between devices  7.75 us (36%)
  Pallas kernels  5.36 us (25%)
    ppermute x6, starting transfers between devices, send(): lax.ppermute(value, axes, [(number[d], number[to(*d)]) for d in devices])  8.02 us
    ppermute x6, waiting for transfers between devices, send(): lax.ppermute(value, axes, [(number[d], number[to(*d)]) for d in devices])  7.75 us
    pallas_call x1, Pallas kernels, local_cross(): pl.pallas_call(spectra_kernel, out_shape=[jax.ShapeDtypeStruct((BLOCK * w...  3.65 us
    pallas_call x4, Pallas kernels, in_vmem(): pl.pallas_call(kernel, out_shape=out_shape, in_specs=[smem] * scalars + [...  1.71 us
  transfers between devices with their start and end apart: 6, of which 5 were waited for; matrix products, arithmetic and copies ran while one was open for 0% of the time, Pallas kernels for 0%

profile of v3, /device:TPU:0, one launch (start us, length us, event | category | flops | bytes accessed | tf_op | source)
XLA Modules:
  0.0 21.2 jit_solution(9797998089184430351)
XLA Ops:
  0.0 0.1 pad_add_fusion.place_ref
  0.1 3.6 %shard_map.55 = (bf16[192,768]{1,0:T(8,128)(2,1)S(1)}, bf16[64,768]{1,0:T(8,128)(2,1)S(1)}) custom-call(s32[2]{0:T(128)S(1)} %pad_add_fusion.place_ref, s32[4]{0:T(128)} %ids_hbm.1, bf16[4,256,512]{2,1,0:T(8,128)(2,1)} %rec_hbm.1, f32[1,65]{1,0:T(1,128)} %bitcast.3, bf16[512,256]{1,0:T(8,128)(2,1)} %constant.13.clone.dft_hbm), custom_call_target="tpu_custom_call" | custom-call | tf_op jit(solution)/shard_map/pallas_call | solution.py:209
  3.7 0.5 %collective-permute-start = (bf16[192,768]{1,0:T(8,128)(2,1)S(1)}, bf16[192,768]{1,0:T(8,128)(2,1)S(1)}, u32[]{:S(2)}, u32[]{:S(2)}) collective-permute-start(bf16[192,768]{1,0:T(8,128)(2,1)S(1)} %get-tuple-element.11.own), channel_id=1, source_target_pairs={{0,1},{1,0},{2,3},{3,2},{4,5},{5,4},{6,7},{7,6},{8,9},{9,8},{10,11... | collective-permute-start | bytes 884744 | tf_op jit(solution)/shard_map/ppermute | solution.py:309
  4.3 1.2 %collective-permute-done.other = bf16[192,768]{1,0:T(8,128)(2,1)S(1)} collective-permute-done((bf16[192,768]{1,0:T(8,128)(2,1)S(1)}, bf16[192,768]{1,0:T(8,128)(2,1)S(1)}, u32[]{:S(2)}, u32[]{:S(2)}) %collective-permute-start) | collective-permute-done | bytes 294944 | tf_op jit(solution)/shard_map/ppermute | solution.py:309
  5.5 0.1 shard_map.56
  5.5 5.0 %collective-permute-start.1 = (bf16[32,768]{1,0:T(8,128)(2,1)S(1)}, bf16[32,768]{1,0:T(8,128)(2,1)S(1)}, u32[]{:S(2)}, u32[]{:S(2)}) collective-permute-start(bf16[32,768]{1,0:T(8,128)(2,1)S(1)} %get-tuple-element.14), channel_id=1, source_target_pairs={{0,12},{1,13},{2,14},{3,15},{4,8},{5,9},{6,10},{7,11},{8,4},{9,5},... | collective-permute-start | bytes 147464 | tf_op jit(solution)/shard_map/ppermute | solution.py:309
  10.6 0.0 collective-permute-start.3
  10.6 0.6 %collective-permute-start.4 = (bf16[64,768]{1,0:T(8,128)(2,1)S(1)}, bf16[64,768]{1,0:T(8,128)(2,1)S(1)}, u32[]{:S(2)}, u32[]{:S(2)}) collective-permute-start(bf16[64,768]{1,0:T(8,128)(2,1)S(1)} %get-tuple-element.16), channel_id=1, source_target_pairs={{0,4},{1,7},{2,6},{3,5},{4,0},{5,3},{6,2},{7,1},{8,12},{9,15},{10,... | collective-permute-start | bytes 294920 | tf_op jit(solution)/shard_map/ppermute | solution.py:309
  11.2 1.5 %collective-permute-done.1.refs_1_ = bf16[32,768]{1,0:T(8,128)(2,1)S(1)} collective-permute-done((bf16[32,768]{1,0:T(8,128)(2,1)S(1)}, bf16[32,768]{1,0:T(8,128)(2,1)S(1)}, u32[]{:S(2)}, u32[]{:S(2)}) %collective-permute-start.1) | collective-permute-done | bytes 49184 | tf_op jit(solution)/shard_map/ppermute | solution.py:309
  12.7 0.0 copy-start
  12.7 1.8 %collective-permute-start.2 = (bf16[32,768]{1,0:T(8,128)(2,1)S(1)}, bf16[32,768]{1,0:T(8,128)(2,1)S(1)}, u32[]{:S(2)}, u32[]{:S(2)}) collective-permute-start(bf16[32,768]{1,0:T(8,128)(2,1)S(1)} %shard_map.57.refs_0_), channel_id=1, source_target_pairs={{0,2},{1,3},{2,0},{3,1},{4,6},{5,7},{6,4},{7,5},{8,10},{9,11},{10,... | collective-permute-start | bytes 147464 | tf_op jit(solution)/shard_map/ppermute | solution.py:309
  14.5 2.9 %collective-permute-done.2.refs_1_ = bf16[32,768]{1,0:T(8,128)(2,1)S(1)} collective-permute-done((bf16[32,768]{1,0:T(8,128)(2,1)S(1)}, bf16[32,768]{1,0:T(8,128)(2,1)S(1)}, u32[]{:S(2)}, u32[]{:S(2)}) %collective-permute-start.2) | collective-permute-done | bytes 49184 | tf_op jit(solution)/shard_map/ppermute | solution.py:309
  17.4 0.7 %collective-permute-done.3.refs_2_ = bf16[64,768]{1,0:T(8,128)(2,1)S(1)} collective-permute-done((bf16[64,768]{1,0:T(8,128)(2,1)S(1)}, bf16[64,768]{1,0:T(8,128)(2,1)S(1)}, u32[]{:S(2)}, u32[]{:S(2)}) %collective-permute-start.3) | collective-permute-done | bytes 98336 | tf_op jit(solution)/shard_map/ppermute | solution.py:309
  18.2 0.0 collective-permute-done.4.refs_3_
  18.2 0.1 collective-permute-start.5
  18.3 1.4 %collective-permute-done.5.other = bf16[96,768]{1,0:T(8,128)(2,1)S(1)} collective-permute-done((bf16[96,768]{1,0:T(8,128)(2,1)S(1)}, bf16[96,768]{1,0:T(8,128)(2,1)S(1)}, u32[]{:S(2)}, u32[]{:S(2)}) %collective-permute-start.5) | collective-permute-done | bytes 147488 | tf_op jit(solution)/shard_map/ppermute | solution.py:309
  19.6 0.0 copy-done
  19.6 1.6 %shard_map.59 = f32[4,64,256]{2,1,0:T(8,128)} custom-call(s32[2]{0:T(128)S(1)} %pad_add_fusion.place_ref, bf16[512,256]{1,0:T(8,128)(2,1)S(1)} %copy-done, bf16[96,768]{1,0:T(8,128)(2,1)S(1)} %shard_map.58.own, bf16[96,768]{1,0:T(8,128)(2,1)S(1)} %collective-permute-done.5.other), custom_call_target="tpu_custom_call" | custom-call | tf_op jit(solution)/shard_map/pallas_call | solution.py:290
  (2 shorter events, 0.1 us)
Async XLA Ops:
  3.7 1.7 %collective-permute-start = (bf16[192,768]{1,0:T(8,128)(2,1)S(1)}, bf16[192,768]{1,0:T(8,128)(2,1)S(1)}, u32[]{:S(2)}, u32[]{:S(2)}) collective-permute-start(bf16[192,768]{1,0:T(8,128)(2,1)S(1)} %get-tuple-element.11.own), channel_id=1, source_target_pairs={{0,1},{1,0},{2,3},{3,2},{4,5},{5,4},{6,7},{7,6},{8,9},{9,8},{10,11... | collective-permute-start | bytes 884744 | tf_op jit(solution)/shard_map/ppermute | solution.py:309
  5.5 7.2 %collective-permute-start.1 = (bf16[32,768]{1,0:T(8,128)(2,1)S(1)}, bf16[32,768]{1,0:T(8,128)(2,1)S(1)}, u32[]{:S(2)}, u32[]{:S(2)}) collective-permute-start(bf16[32,768]{1,0:T(8,128)(2,1)S(1)} %get-tuple-element.14), channel_id=1, source_target_pairs={{0,12},{1,13},{2,14},{3,15},{4,8},{5,9},{6,10},{7,11},{8,4},{9,5},... | collective-permute-start | bytes 147464 | tf_op jit(solution)/shard_map/ppermute | solution.py:309
  10.6 7.6 %collective-permute-start.3 = (bf16[64,768]{1,0:T(8,128)(2,1)S(1)}, bf16[64,768]{1,0:T(8,128)(2,1)S(1)}, u32[]{:S(2)}, u32[]{:S(2)}) collective-permute-start(bf16[64,768]{1,0:T(8,128)(2,1)S(1)} %get-tuple-element.15), channel_id=1, source_target_pairs={{0,8},{1,11},{2,10},{3,9},{4,12},{5,15},{6,14},{7,13},{8,0},{9,3},... | collective-permute-start | bytes 294920 | tf_op jit(solution)/shard_map/ppermute | solution.py:309
  10.6 7.6 %collective-permute-start.4 = (bf16[64,768]{1,0:T(8,128)(2,1)S(1)}, bf16[64,768]{1,0:T(8,128)(2,1)S(1)}, u32[]{:S(2)}, u32[]{:S(2)}) collective-permute-start(bf16[64,768]{1,0:T(8,128)(2,1)S(1)} %get-tuple-element.16), channel_id=1, source_target_pairs={{0,4},{1,7},{2,6},{3,5},{4,0},{5,3},{6,2},{7,1},{8,12},{9,15},{10,... | collective-permute-start | bytes 294920 | tf_op jit(solution)/shard_map/ppermute | solution.py:309
  12.7 6.9 %copy-start = (bf16[512,256]{1,0:T(8,128)(2,1)S(1)}, bf16[512,256]{1,0:T(8,128)(2,1)}, u32[]{:S(2)}) copy-start(bf16[512,256]{1,0:T(8,128)(2,1)} %constant.14.clone.table_ref) | copy-start | bytes 786436
  12.7 4.7 %collective-permute-start.2 = (bf16[32,768]{1,0:T(8,128)(2,1)S(1)}, bf16[32,768]{1,0:T(8,128)(2,1)S(1)}, u32[]{:S(2)}, u32[]{:S(2)}) collective-permute-start(bf16[32,768]{1,0:T(8,128)(2,1)S(1)} %shard_map.57.refs_0_), channel_id=1, source_target_pairs={{0,2},{1,3},{2,0},{3,1},{4,6},{5,7},{6,4},{7,5},{8,10},{9,11},{10,... | collective-permute-start | bytes 147464 | tf_op jit(solution)/shard_map/ppermute | solution.py:309
  18.2 1.4 %collective-permute-start.5 = (bf16[96,768]{1,0:T(8,128)(2,1)S(1)}, bf16[96,768]{1,0:T(8,128)(2,1)S(1)}, u32[]{:S(2)}, u32[]{:S(2)}) collective-permute-start(bf16[96,768]{1,0:T(8,128)(2,1)S(1)} %shard_map.58.own), channel_id=1, source_target_pairs={{0,1},{1,0},{2,3},{3,2},{4,5},{5,4},{6,7},{7,6},{8,9},{9,8},{10,11... | collective-permute-start | bytes 442376 | tf_op jit(solution)/shard_map/ppermute | solution.py:309

commit v4 on v3

--- a/solution.py
+++ b/solution.py
@@ -79,7 +79,6 @@
 
 
 def spectra_kernel(
-    place_ref,
     ids_hbm,
     rec_hbm,
     taps_hbm,
@@ -161,17 +160,17 @@
                 unit.astype(jnp.float32).reshape(windows, width, LANES), axis=1
             )
 
-    def cross(k, rows):
-        b = relative(place_ref[0], k, blocks)
+    def cross(k):
+        b = relative(lax.axis_index("chan"), k, blocks)
         re, im = [], []
         for s in range(count):
-            total_re = jnp.zeros((rows.size, LANES), jnp.float32)
-            total_im = jnp.zeros((rows.size, LANES), jnp.float32)
+            total_re = jnp.zeros((width, LANES), jnp.float32)
+            total_im = jnp.zeros((width, LANES), jnp.float32)
             for w in range(windows):
                 src_re = sums[0, ids_ref[s], w : w + 1, :]
                 src_im = sums[1, ids_ref[s], w : w + 1, :]
-                white_re = white[0, b, w, rows, :].astype(jnp.float32)
-                white_im = white[1, b, w, rows, :].astype(jnp.float32)
+                white_re = white[0, b, w].astype(jnp.float32)
+                white_im = white[1, b, w].astype(jnp.float32)
                 total_re += white_re * src_re + white_im * src_im
                 total_im += white_im * src_re - white_re * src_im
             re.append(total_re)
@@ -180,14 +179,15 @@
 
     whole, shared = kinds(blocks)
     half = width // 2
-    mine = pl.ds(pl.multiple_of(place_ref[1] * half, half), half)
-    theirs = pl.ds(pl.multiple_of((1 - place_ref[1]) * half, half), half)
+    first = lax.axis_index("rep") == 0
     for i, k in enumerate(whole):
-        out_ref[width * i : width * (i + 1), :] = cross(k, pl.ds(0, width))
+        out_ref[width * i : width * (i + 1), :] = cross(k)
     for i, k in enumerate(shared):
         start = width * len(whole) + half * i
-        out_ref[start : start + half, :] = cross(k, theirs)
-        kept_ref[half * i : half * (i + 1), :] = cross(k, mine)
+        value = cross(k)
+        top, bottom = value[:half], value[half:]
+        out_ref[start : start + half, :] = jnp.where(first, bottom, top)
+        kept_ref[half * i : half * (i + 1), :] = jnp.where(first, top, bottom)
 
 
 def kinds(blocks):
@@ -200,7 +200,7 @@
     return (me + k) % size
 
 
-def local_cross(place, source_ids, records, taps, dft):
+def local_cross(source_ids, records, taps, dft):
     windows, channels, samples = records.shape
     blocks = channels // BLOCK
     whole, shared = (len(kind) for kind in kinds(blocks))
@@ -212,7 +212,7 @@
             jax.ShapeDtypeStruct((BLOCK * whole + half * shared, 6 * LANES), jnp.bfloat16),
             jax.ShapeDtypeStruct((half * shared, 6 * LANES), jnp.bfloat16),
         ],
-        in_specs=[pl.BlockSpec(memory_space=pltpu.SMEM), hbm, hbm, hbm, hbm],
+        in_specs=[hbm] * 4,
         out_specs=[pl.BlockSpec(memory_space=pltpu.VMEM)] * 2,
         scratch_shapes=[
             pltpu.SMEM(source_ids.shape, jnp.int32),
@@ -228,7 +228,7 @@
             pltpu.SemaphoreType.DMA((blocks,)),
         ],
         compiler_params=pltpu.CompilerParams(vmem_limit_bytes=VMEM_LIMIT),
-    )(place, *(pltpu.with_memory_space_constraint(v, pltpu.HBM) for v in (source_ids, records, taps, dft)))
+    )(*(pltpu.with_memory_space_constraint(v, pltpu.HBM) for v in (source_ids, records, taps, dft)))
 
 
 def tree(values):
@@ -267,14 +267,15 @@
     out[rows:, :] = share.astype(out.dtype)
 
 
-def lag_kernel(scale, place_ref, table_ref, own, other, out, total):
-    rows = total.shape[0]
-    half = rows // 2
-    total[...] = own[:rows, :].astype(jnp.float32) + other[:rows, :].astype(jnp.float32)
-    for core, ref in ((place_ref[1], own), (1 - place_ref[1], other)):
-        at = pl.ds(pl.multiple_of(core * half, half), half)
-        total[at, :] += ref[rows:, :].astype(jnp.float32)
-    cross = unpack(total[...])
+def lag_kernel(scale, table_ref, own, other, out):
+    rows = out.shape[1]
+    first = lax.axis_index("rep") == 0
+    mine, theirs = own[rows:, :].astype(jnp.float32), other[rows:, :].astype(jnp.float32)
+    shares = jnp.concatenate(
+        [jnp.where(first, mine, theirs), jnp.where(first, theirs, mine)], axis=0
+    )
+    total = own[:rows, :].astype(jnp.float32) + other[:rows, :].astype(jnp.float32) + shares
+    cross = unpack(total)
     high = cross.astype(jnp.bfloat16)
     low = (cross - high.astype(jnp.float32)).astype(jnp.bfloat16)
     dot = functools.partial(jnp.dot, preferred_element_type=jnp.float32)
@@ -283,16 +284,14 @@
     out[...] = (scale * lags).reshape(out.shape)
 
 
-def in_vmem(kernel, out_shape, inputs, scalars=0, scratch=()):
+def in_vmem(kernel, out_shape, inputs):
     vmem = pl.BlockSpec(memory_space=pltpu.VMEM)
-    smem = pl.BlockSpec(memory_space=pltpu.SMEM)
     several = isinstance(out_shape, list)
     return pl.pallas_call(
         kernel,
         out_shape=out_shape,
-        in_specs=[smem] * scalars + [vmem] * (len(inputs) - scalars),
+        in_specs=[vmem] * len(inputs),
         out_specs=[vmem] * len(out_shape) if several else vmem,
-        scratch_shapes=scratch,
         compiler_params=pltpu.CompilerParams(vmem_limit_bytes=VMEM_LIMIT),
     )(*inputs)
 
@@ -308,9 +307,8 @@
     def send(value, to):
         return lax.ppermute(value, axes, [(number[d], number[to(*d)]) for d in devices])
 
-    place = jnp.stack([lax.axis_index("chan"), lax.axis_index("rep")]).astype(jnp.int32)
     own, kept = local_cross(
-        place, source_ids, records, fir_taps.reshape(1, -1), jnp.asarray(dft_table(samples))
+        source_ids, records, fir_taps.reshape(1, -1), jnp.asarray(dft_table(samples))
     )
     width, half = 6 * LANES, BLOCK // 2
     whole, shared = kinds(chans)
@@ -346,9 +344,7 @@
     return in_vmem(
         functools.partial(lag_kernel, scale),
         jax.ShapeDtypeStruct((source_ids.shape[0], BLOCK, LAGS), jnp.float32),
-        [place, jnp.asarray(lag_table(samples)), total, other],
-        scalars=1,
-        scratch=[pltpu.VMEM((BLOCK, width), jnp.float32)],
+        [jnp.asarray(lag_table(samples)), total, other],
     )
 
 

time: 21.4 us -> 20.2 us (0.944)
  Pallas kernels: 5.36 us -> 4.26 us
    pallas_call x4, Pallas kernels: 1.71 us -> 1.13 us  [in_vmem(): pl.pallas_call(kernel, out_shape=out_shape, in_specs=[vmem] * len(inputs)...]
    pallas_call x1, Pallas kernels: 3.65 us -> 3.13 us  [local_cross(): pl.pallas_call(spectra_kernel, out_shape=[jax.ShapeDtypeStruct((BLOCK * w...]
where the time goes in v4:
time: 20.2 us; the launch traced here: 20.1 us
  starting transfers between devices  8.02 us (40%)
  waiting for transfers between devices  7.75 us (38%)
  Pallas kernels  4.26 us (21%)
    ppermute x6, starting transfers between devices, send(): lax.ppermute(value, axes, [(number[d], number[to(*d)]) for d in devices])  8.02 us
    ppermute x6, waiting for transfers between devices, send(): lax.ppermute(value, axes, [(number[d], number[to(*d)]) for d in devices])  7.75 us
    pallas_call x1, Pallas kernels, local_cross(): pl.pallas_call(spectra_kernel, out_shape=[jax.ShapeDtypeStruct((BLOCK * w...  3.13 us
    pallas_call x4, Pallas kernels, in_vmem(): pl.pallas_call(kernel, out_shape=out_shape, in_specs=[vmem] * len(inputs)...  1.13 us
  transfers between devices with their start and end apart: 6, of which 5 were waited for; matrix products, arithmetic and copies ran while one was open for 0% of the time, Pallas kernels for 0%

profile of v4, /device:TPU:0, one launch (start us, length us, event | category | flops | bytes accessed | tf_op | source)
XLA Modules:
  0.0 20.1 jit_solution(5890555869330841720)
XLA Ops:
  0.0 3.1 %shard_map.55 = (bf16[192,768]{1,0:T(8,128)(2,1)S(1)}, bf16[64,768]{1,0:T(8,128)(2,1)S(1)}) custom-call(s32[4]{0:T(128)} %ids_hbm.1, bf16[4,256,512]{2,1,0:T(8,128)(2,1)} %rec_hbm.1, f32[1,65]{1,0:T(1,128)} %bitcast.1, bf16[512,256]{1,0:T(8,128)(2,1)} %constant.4.clone.dft_hbm), custom_call_target="tpu_custom_call" | custom-call | tf_op jit(solution)/shard_map/pallas_call | solution.py:209
  3.1 0.5 %collective-permute-start = (bf16[192,768]{1,0:T(8,128)(2,1)S(1)}, bf16[192,768]{1,0:T(8,128)(2,1)S(1)}, u32[]{:S(2)}, u32[]{:S(2)}) collective-permute-start(bf16[192,768]{1,0:T(8,128)(2,1)S(1)} %get-tuple-element.11.own), channel_id=1, source_target_pairs={{0,1},{1,0},{2,3},{3,2},{4,5},{5,4},{6,7},{7,6},{8,9},{9,8},{10,11... | collective-permute-start | bytes 884744 | tf_op jit(solution)/shard_map/ppermute | solution.py:308
  3.7 1.2 %collective-permute-done.other = bf16[192,768]{1,0:T(8,128)(2,1)S(1)} collective-permute-done((bf16[192,768]{1,0:T(8,128)(2,1)S(1)}, bf16[192,768]{1,0:T(8,128)(2,1)S(1)}, u32[]{:S(2)}, u32[]{:S(2)}) %collective-permute-start) | collective-permute-done | bytes 294944 | tf_op jit(solution)/shard_map/ppermute | solution.py:308
  4.9 0.1 shard_map.56
  4.9 5.0 %collective-permute-start.1 = (bf16[32,768]{1,0:T(8,128)(2,1)S(1)}, bf16[32,768]{1,0:T(8,128)(2,1)S(1)}, u32[]{:S(2)}, u32[]{:S(2)}) collective-permute-start(bf16[32,768]{1,0:T(8,128)(2,1)S(1)} %get-tuple-element.14), channel_id=1, source_target_pairs={{0,12},{1,13},{2,14},{3,15},{4,8},{5,9},{6,10},{7,11},{8,4},{9,5},... | collective-permute-start | bytes 147464 | tf_op jit(solution)/shard_map/ppermute | solution.py:308
  10.0 0.0 collective-permute-start.3
  10.0 0.6 %collective-permute-start.4 = (bf16[64,768]{1,0:T(8,128)(2,1)S(1)}, bf16[64,768]{1,0:T(8,128)(2,1)S(1)}, u32[]{:S(2)}, u32[]{:S(2)}) collective-permute-start(bf16[64,768]{1,0:T(8,128)(2,1)S(1)} %get-tuple-element.16), channel_id=1, source_target_pairs={{0,4},{1,7},{2,6},{3,5},{4,0},{5,3},{6,2},{7,1},{8,12},{9,15},{10,... | collective-permute-start | bytes 294920 | tf_op jit(solution)/shard_map/ppermute | solution.py:308
  10.6 1.5 %collective-permute-done.1.refs_1_ = bf16[32,768]{1,0:T(8,128)(2,1)S(1)} collective-permute-done((bf16[32,768]{1,0:T(8,128)(2,1)S(1)}, bf16[32,768]{1,0:T(8,128)(2,1)S(1)}, u32[]{:S(2)}, u32[]{:S(2)}) %collective-permute-start.1) | collective-permute-done | bytes 49184 | tf_op jit(solution)/shard_map/ppermute | solution.py:308
  12.1 0.0 copy-start
  12.1 1.8 %collective-permute-start.2 = (bf16[32,768]{1,0:T(8,128)(2,1)S(1)}, bf16[32,768]{1,0:T(8,128)(2,1)S(1)}, u32[]{:S(2)}, u32[]{:S(2)}) collective-permute-start(bf16[32,768]{1,0:T(8,128)(2,1)S(1)} %shard_map.57.refs_0_), channel_id=1, source_target_pairs={{0,2},{1,3},{2,0},{3,1},{4,6},{5,7},{6,4},{7,5},{8,10},{9,11},{10,... | collective-permute-start | bytes 147464 | tf_op jit(solution)/shard_map/ppermute | solution.py:308
  13.9 2.9 %collective-permute-done.2.refs_1_ = bf16[32,768]{1,0:T(8,128)(2,1)S(1)} collective-permute-done((bf16[32,768]{1,0:T(8,128)(2,1)S(1)}, bf16[32,768]{1,0:T(8,128)(2,1)S(1)}, u32[]{:S(2)}, u32[]{:S(2)}) %collective-permute-start.2) | collective-permute-done | bytes 49184 | tf_op jit(solution)/shard_map/ppermute | solution.py:308
  16.8 0.7 %collective-permute-done.3.refs_2_ = bf16[64,768]{1,0:T(8,128)(2,1)S(1)} collective-permute-done((bf16[64,768]{1,0:T(8,128)(2,1)S(1)}, bf16[64,768]{1,0:T(8,128)(2,1)S(1)}, u32[]{:S(2)}, u32[]{:S(2)}) %collective-permute-start.3) | collective-permute-done | bytes 98336 | tf_op jit(solution)/shard_map/ppermute | solution.py:308
  17.6 0.0 collective-permute-done.4.refs_3_
  17.6 0.1 collective-permute-start.5
  17.7 1.4 %collective-permute-done.5.other = bf16[96,768]{1,0:T(8,128)(2,1)S(1)} collective-permute-done((bf16[96,768]{1,0:T(8,128)(2,1)S(1)}, bf16[96,768]{1,0:T(8,128)(2,1)S(1)}, u32[]{:S(2)}, u32[]{:S(2)}) %collective-permute-start.5) | collective-permute-done | bytes 147488 | tf_op jit(solution)/shard_map/ppermute | solution.py:308
  19.0 0.0 copy-done
  19.0 1.0 %shard_map.59 = f32[4,64,256]{2,1,0:T(8,128)} custom-call(bf16[512,256]{1,0:T(8,128)(2,1)S(1)} %copy-done, bf16[96,768]{1,0:T(8,128)(2,1)S(1)} %shard_map.58.own, bf16[96,768]{1,0:T(8,128)(2,1)S(1)} %collective-permute-done.5.other), custom_call_target="tpu_custom_call" | custom-call | tf_op jit(solution)/shard_map/pallas_call | solution.py:290
  (2 shorter events, 0.1 us)
Async XLA Ops:
  3.1 1.7 %collective-permute-start = (bf16[192,768]{1,0:T(8,128)(2,1)S(1)}, bf16[192,768]{1,0:T(8,128)(2,1)S(1)}, u32[]{:S(2)}, u32[]{:S(2)}) collective-permute-start(bf16[192,768]{1,0:T(8,128)(2,1)S(1)} %get-tuple-element.11.own), channel_id=1, source_target_pairs={{0,1},{1,0},{2,3},{3,2},{4,5},{5,4},{6,7},{7,6},{8,9},{9,8},{10,11... | collective-permute-start | bytes 884744 | tf_op jit(solution)/shard_map/ppermute | solution.py:308
  4.9 7.2 %collective-permute-start.1 = (bf16[32,768]{1,0:T(8,128)(2,1)S(1)}, bf16[32,768]{1,0:T(8,128)(2,1)S(1)}, u32[]{:S(2)}, u32[]{:S(2)}) collective-permute-start(bf16[32,768]{1,0:T(8,128)(2,1)S(1)} %get-tuple-element.14), channel_id=1, source_target_pairs={{0,12},{1,13},{2,14},{3,15},{4,8},{5,9},{6,10},{7,11},{8,4},{9,5},... | collective-permute-start | bytes 147464 | tf_op jit(solution)/shard_map/ppermute | solution.py:308
  10.0 7.6 %collective-permute-start.3 = (bf16[64,768]{1,0:T(8,128)(2,1)S(1)}, bf16[64,768]{1,0:T(8,128)(2,1)S(1)}, u32[]{:S(2)}, u32[]{:S(2)}) collective-permute-start(bf16[64,768]{1,0:T(8,128)(2,1)S(1)} %get-tuple-element.15), channel_id=1, source_target_pairs={{0,8},{1,11},{2,10},{3,9},{4,12},{5,15},{6,14},{7,13},{8,0},{9,3},... | collective-permute-start | bytes 294920 | tf_op jit(solution)/shard_map/ppermute | solution.py:308
  10.0 7.6 %collective-permute-start.4 = (bf16[64,768]{1,0:T(8,128)(2,1)S(1)}, bf16[64,768]{1,0:T(8,128)(2,1)S(1)}, u32[]{:S(2)}, u32[]{:S(2)}) collective-permute-start(bf16[64,768]{1,0:T(8,128)(2,1)S(1)} %get-tuple-element.16), channel_id=1, source_target_pairs={{0,4},{1,7},{2,6},{3,5},{4,0},{5,3},{6,2},{7,1},{8,12},{9,15},{10,... | collective-permute-start | bytes 294920 | tf_op jit(solution)/shard_map/ppermute | solution.py:308
  12.1 6.9 %copy-start = (bf16[512,256]{1,0:T(8,128)(2,1)S(1)}, bf16[512,256]{1,0:T(8,128)(2,1)}, u32[]{:S(2)}) copy-start(bf16[512,256]{1,0:T(8,128)(2,1)} %constant.5.clone.table_ref) | copy-start | bytes 786436
  12.1 4.7 %collective-permute-start.2 = (bf16[32,768]{1,0:T(8,128)(2,1)S(1)}, bf16[32,768]{1,0:T(8,128)(2,1)S(1)}, u32[]{:S(2)}, u32[]{:S(2)}) collective-permute-start(bf16[32,768]{1,0:T(8,128)(2,1)S(1)} %shard_map.57.refs_0_), channel_id=1, source_target_pairs={{0,2},{1,3},{2,0},{3,1},{4,6},{5,7},{6,4},{7,5},{8,10},{9,11},{10,... | collective-permute-start | bytes 147464 | tf_op jit(solution)/shard_map/ppermute | solution.py:308
  17.6 1.4 %collective-permute-start.5 = (bf16[96,768]{1,0:T(8,128)(2,1)S(1)}, bf16[96,768]{1,0:T(8,128)(2,1)S(1)}, u32[]{:S(2)}, u32[]{:S(2)}) collective-permute-start(bf16[96,768]{1,0:T(8,128)(2,1)S(1)} %shard_map.58.own), channel_id=1, source_target_pairs={{0,1},{1,0},{2,3},{3,2},{4,5},{5,4},{6,7},{7,6},{8,9},{9,8},{10,11... | collective-permute-start | bytes 442376 | tf_op jit(solution)/shard_map/ppermute | solution.py:308

commit v5 on v4

--- a/solution.py
+++ b/solution.py
@@ -191,12 +191,10 @@
 
 
 def kinds(blocks):
-    return list(range(3 * blocks // 4 - 1, 0, -1)), list(range(3 * blocks // 4, blocks)) + [0]
+    return list(range(1, blocks // 2)), list(range(blocks // 2, blocks)) + [0]
 
 
 def relative(me, k, size):
-    if size & (size - 1) == 0:
-        return me ^ k
     return (me + k) % size
 
 
@@ -299,7 +297,7 @@
 def body(records, fir_taps, source_ids):
     samples = records.shape[2]
     chans, times, cores = (lax.axis_size(axis) for axis in ("chan", "tm", "rep"))
-    assert cores == 2
+    assert cores == 2 and times & (times - 1) == 0
     axes = ("chan", "tm", "rep")
     devices = [(a, t, r) for a in range(chans) for t in range(times) for r in range(cores)]
     number = {device: i for i, device in enumerate(devices)}
@@ -325,13 +323,13 @@
         for k, piece in zip(shared[:-1], pieces[len(whole) :])
     ]
     arrived = [
-        send(piece, lambda a, t, r, k=k: (relative(a, k, chans), relative(t, turn + r, times), r))
+        send(piece, lambda a, t, r, k=k: (relative(a, k, chans), t ^ (turn + r), r))
         for k, piece in zip(whole, pieces)
         for turn in range(0, times, cores)
     ]
     share = in_vmem(tree_kernel, part, [pieces[-1]] + shares)
     shares = [share] + [
-        send(share, lambda a, t, r, j=j: (a, relative(t, j, times), r)) for j in range(1, times)
+        send(share, lambda a, t, r, j=j: (a, t ^ j, r)) for j in range(1, times)
     ]
     total = in_vmem(
         functools.partial(core_kernel, -(-times // cores), times),

time: 20.2 us -> 19.9 us (0.985)
  waiting for transfers between devices: 7.75 us -> 7.24 us
    ppermute x6, waiting for transfers between devices: 7.75 us -> 7.24 us  [send(): lax.ppermute(value, axes, [(number[d], number[to(*d)]) for d in devices])]
  transfers between devices with their start and end apart: 6 -> 6, of which waited for: 5 -> 6; matrix products, arithmetic and copies ran while one was open for 0% -> 0% of each run, Pallas kernels for 0% -> 0%
where the time goes in v5:
time: 19.9 us; the launch traced here: 19.7 us
  starting transfers between devices  8.2 us (41%)
  waiting for transfers between devices  7.24 us (36%)
  Pallas kernels  4.25 us (21%)
    ppermute x6, starting transfers between devices, send(): lax.ppermute(value, axes, [(number[d], number[to(*d)]) for d in devices])  8.2 us
    ppermute x6, waiting for transfers between devices, send(): lax.ppermute(value, axes, [(number[d], number[to(*d)]) for d in devices])  7.24 us
    pallas_call x1, Pallas kernels, local_cross(): pl.pallas_call(spectra_kernel, out_shape=[jax.ShapeDtypeStruct((BLOCK * w...  3.14 us
    pallas_call x4, Pallas kernels, in_vmem(): pl.pallas_call(kernel, out_shape=out_shape, in_specs=[vmem] * len(inputs)...  1.11 us
  transfers between devices with their start and end apart: 6, of which 6 were waited for; matrix products, arithmetic and copies ran while one was open for 0% of the time, Pallas kernels for 0%

profile of v5, /device:TPU:0, one launch (start us, length us, event | category | flops | bytes accessed | tf_op | source)
XLA Modules:
  0.0 19.7 jit_solution(559324065251987064)
XLA Ops:
  0.0 3.1 %shard_map.55 = (bf16[160,768]{1,0:T(8,128)(2,1)S(1)}, bf16[96,768]{1,0:T(8,128)(2,1)S(1)}) custom-call(s32[4]{0:T(128)} %ids_hbm.1, bf16[4,256,512]{2,1,0:T(8,128)(2,1)} %rec_hbm.1, f32[1,65]{1,0:T(1,128)} %bitcast.1, bf16[512,256]{1,0:T(8,128)(2,1)} %constant.4.clone.dft_hbm), custom_call_target="tpu_custom_call" | custom-call | tf_op jit(solution)/shard_map/pallas_call | solution.py:207
  3.1 0.5 %collective-permute-start = (bf16[160,768]{1,0:T(8,128)(2,1)S(1)}, bf16[160,768]{1,0:T(8,128)(2,1)S(1)}, u32[]{:S(2)}, u32[]{:S(2)}) collective-permute-start(bf16[160,768]{1,0:T(8,128)(2,1)S(1)} %get-tuple-element.11.own), channel_id=1, source_target_pairs={{0,1},{1,0},{2,3},{3,2},{4,5},{5,4},{6,7},{7,6},{8,9},{9,8},{10,11... | collective-permute-start | bytes 737288 | tf_op jit(solution)/shard_map/ppermute | solution.py:306
  3.7 1.1 %collective-permute-done.other = bf16[160,768]{1,0:T(8,128)(2,1)S(1)} collective-permute-done((bf16[160,768]{1,0:T(8,128)(2,1)S(1)}, bf16[160,768]{1,0:T(8,128)(2,1)S(1)}, u32[]{:S(2)}, u32[]{:S(2)}) %collective-permute-start) | collective-permute-done | bytes 245792 | tf_op jit(solution)/shard_map/ppermute | solution.py:306
  4.8 0.1 shard_map.56
  4.9 4.0 %collective-permute-start.1 = (bf16[32,768]{1,0:T(8,128)(2,1)S(1)}, bf16[32,768]{1,0:T(8,128)(2,1)S(1)}, u32[]{:S(2)}, u32[]{:S(2)}) collective-permute-start(bf16[32,768]{1,0:T(8,128)(2,1)S(1)} %get-tuple-element.14), channel_id=1, source_target_pairs={{0,8},{1,9},{2,10},{3,11},{4,12},{5,13},{6,14},{7,15},{8,0},{9,1},... | collective-permute-start | bytes 147464 | tf_op jit(solution)/shard_map/ppermute | solution.py:306
  8.9 1.3 %collective-permute-start.2 = (bf16[32,768]{1,0:T(8,128)(2,1)S(1)}, bf16[32,768]{1,0:T(8,128)(2,1)S(1)}, u32[]{:S(2)}, u32[]{:S(2)}) collective-permute-start(bf16[32,768]{1,0:T(8,128)(2,1)S(1)} %get-tuple-element.15), channel_id=1, source_target_pairs={{0,12},{1,13},{2,14},{3,15},{4,0},{5,1},{6,2},{7,3},{8,4},{9,5},{1... | collective-permute-start | bytes 147464 | tf_op jit(solution)/shard_map/ppermute | solution.py:306
  10.2 0.7 %collective-permute-start.4 = (bf16[64,768]{1,0:T(8,128)(2,1)S(1)}, bf16[64,768]{1,0:T(8,128)(2,1)S(1)}, u32[]{:S(2)}, u32[]{:S(2)}) collective-permute-start(bf16[64,768]{1,0:T(8,128)(2,1)S(1)} %get-tuple-element.16), channel_id=1, source_target_pairs={{0,4},{1,7},{2,6},{3,5},{4,8},{5,11},{6,10},{7,9},{8,12},{9,15},{1... | collective-permute-start | bytes 294920 | tf_op jit(solution)/shard_map/ppermute | solution.py:306
  10.9 0.1 collective-permute-done.1.refs_1_
  11.0 2.0 %collective-permute-done.2.refs_2_ = bf16[32,768]{1,0:T(8,128)(2,1)S(1)} collective-permute-done((bf16[32,768]{1,0:T(8,128)(2,1)S(1)}, bf16[32,768]{1,0:T(8,128)(2,1)S(1)}, u32[]{:S(2)}, u32[]{:S(2)}) %collective-permute-start.2) | collective-permute-done | bytes 49184 | tf_op jit(solution)/shard_map/ppermute | solution.py:306
  13.0 0.0 copy-start
  13.0 1.6 %collective-permute-start.3 = (bf16[32,768]{1,0:T(8,128)(2,1)S(1)}, bf16[32,768]{1,0:T(8,128)(2,1)S(1)}, u32[]{:S(2)}, u32[]{:S(2)}) collective-permute-start(bf16[32,768]{1,0:T(8,128)(2,1)S(1)} %shard_map.57.refs_0_), channel_id=1, source_target_pairs={{0,2},{1,3},{2,0},{3,1},{4,6},{5,7},{6,4},{7,5},{8,10},{9,11},{10,... | collective-permute-start | bytes 147464 | tf_op jit(solution)/shard_map/ppermute | solution.py:306
  14.6 2.6 %collective-permute-done.3.refs_1_ = bf16[32,768]{1,0:T(8,128)(2,1)S(1)} collective-permute-done((bf16[32,768]{1,0:T(8,128)(2,1)S(1)}, bf16[32,768]{1,0:T(8,128)(2,1)S(1)}, u32[]{:S(2)}, u32[]{:S(2)}) %collective-permute-start.3) | collective-permute-done | bytes 49184 | tf_op jit(solution)/shard_map/ppermute | solution.py:306
  17.2 0.1 collective-permute-done.4.refs_2_
  17.3 0.1 collective-permute-start.5
  17.4 1.4 %collective-permute-done.5.other = bf16[96,768]{1,0:T(8,128)(2,1)S(1)} collective-permute-done((bf16[96,768]{1,0:T(8,128)(2,1)S(1)}, bf16[96,768]{1,0:T(8,128)(2,1)S(1)}, u32[]{:S(2)}, u32[]{:S(2)}) %collective-permute-start.5) | collective-permute-done | bytes 147488 | tf_op jit(solution)/shard_map/ppermute | solution.py:306
  18.7 0.0 copy-done
  18.7 1.0 %shard_map.59 = f32[4,64,256]{2,1,0:T(8,128)} custom-call(bf16[512,256]{1,0:T(8,128)(2,1)S(1)} %copy-done, bf16[96,768]{1,0:T(8,128)(2,1)S(1)} %shard_map.58.own, bf16[96,768]{1,0:T(8,128)(2,1)S(1)} %collective-permute-done.5.other), custom_call_target="tpu_custom_call" | custom-call | tf_op jit(solution)/shard_map/pallas_call | solution.py:288
  (2 shorter events, 0.0 us)
Async XLA Ops:
  3.1 1.7 %collective-permute-start = (bf16[160,768]{1,0:T(8,128)(2,1)S(1)}, bf16[160,768]{1,0:T(8,128)(2,1)S(1)}, u32[]{:S(2)}, u32[]{:S(2)}) collective-permute-start(bf16[160,768]{1,0:T(8,128)(2,1)S(1)} %get-tuple-element.11.own), channel_id=1, source_target_pairs={{0,1},{1,0},{2,3},{3,2},{4,5},{5,4},{6,7},{7,6},{8,9},{9,8},{10,11... | collective-permute-start | bytes 737288 | tf_op jit(solution)/shard_map/ppermute | solution.py:306
  4.9 6.1 %collective-permute-start.1 = (bf16[32,768]{1,0:T(8,128)(2,1)S(1)}, bf16[32,768]{1,0:T(8,128)(2,1)S(1)}, u32[]{:S(2)}, u32[]{:S(2)}) collective-permute-start(bf16[32,768]{1,0:T(8,128)(2,1)S(1)} %get-tuple-element.14), channel_id=1, source_target_pairs={{0,8},{1,9},{2,10},{3,11},{4,12},{5,13},{6,14},{7,15},{8,0},{9,1},... | collective-permute-start | bytes 147464 | tf_op jit(solution)/shard_map/ppermute | solution.py:306
  8.9 4.1 %collective-permute-start.2 = (bf16[32,768]{1,0:T(8,128)(2,1)S(1)}, bf16[32,768]{1,0:T(8,128)(2,1)S(1)}, u32[]{:S(2)}, u32[]{:S(2)}) collective-permute-start(bf16[32,768]{1,0:T(8,128)(2,1)S(1)} %get-tuple-element.15), channel_id=1, source_target_pairs={{0,12},{1,13},{2,14},{3,15},{4,0},{5,1},{6,2},{7,3},{8,4},{9,5},{1... | collective-permute-start | bytes 147464 | tf_op jit(solution)/shard_map/ppermute | solution.py:306
  10.2 7.0 %collective-permute-start.4 = (bf16[64,768]{1,0:T(8,128)(2,1)S(1)}, bf16[64,768]{1,0:T(8,128)(2,1)S(1)}, u32[]{:S(2)}, u32[]{:S(2)}) collective-permute-start(bf16[64,768]{1,0:T(8,128)(2,1)S(1)} %get-tuple-element.16), channel_id=1, source_target_pairs={{0,4},{1,7},{2,6},{3,5},{4,8},{5,11},{6,10},{7,9},{8,12},{9,15},{1... | collective-permute-start | bytes 294920 | tf_op jit(solution)/shard_map/ppermute | solution.py:306
  13.0 5.7 %copy-start = (bf16[512,256]{1,0:T(8,128)(2,1)S(1)}, bf16[512,256]{1,0:T(8,128)(2,1)}, u32[]{:S(2)}) copy-start(bf16[512,256]{1,0:T(8,128)(2,1)} %constant.5.clone.table_ref) | copy-start | bytes 786436
  13.0 4.2 %collective-permute-start.3 = (bf16[32,768]{1,0:T(8,128)(2,1)S(1)}, bf16[32,768]{1,0:T(8,128)(2,1)S(1)}, u32[]{:S(2)}, u32[]{:S(2)}) collective-permute-start(bf16[32,768]{1,0:T(8,128)(2,1)S(1)} %shard_map.57.refs_0_), channel_id=1, source_target_pairs={{0,2},{1,3},{2,0},{3,1},{4,6},{5,7},{6,4},{7,5},{8,10},{9,11},{10,... | collective-permute-start | bytes 147464 | tf_op jit(solution)/shard_map/ppermute | solution.py:306
  17.3 1.4 %collective-permute-start.5 = (bf16[96,768]{1,0:T(8,128)(2,1)S(1)}, bf16[96,768]{1,0:T(8,128)(2,1)S(1)}, u32[]{:S(2)}, u32[]{:S(2)}) collective-permute-start(bf16[96,768]{1,0:T(8,128)(2,1)S(1)} %shard_map.58.own), channel_id=1, source_target_pairs={{0,1},{1,0},{2,3},{3,2},{4,5},{5,4},{6,7},{7,6},{8,9},{9,8},{10,11... | collective-permute-start | bytes 442376 | tf_op jit(solution)/shard_map/ppermute | solution.py:306

commit v6 on v5

--- a/solution.py
+++ b/solution.py
@@ -128,16 +128,17 @@
                 :, LANES * (j - i + 1) : LANES * (j - i + 2)
             ]
     copies[2].wait()
-    both_tables = jnp.dot(fir[...], dft_ref[...], preferred_element_type=jnp.float32).astype(
-        jnp.bfloat16
-    )
     copies[1].wait()
     for load in loads:
         load.wait()
-    spectra, both = [], []
+    filtered, spectra, both = [], [], []
     for b in range(blocks):
         block = rec_ref[b].reshape(windows * width, samples)
-        spectra.append(jnp.dot(block, both_tables, preferred_element_type=jnp.float32))
+        filtered.append(
+            jnp.dot(block, fir[...], preferred_element_type=jnp.float32).astype(jnp.bfloat16)
+        )
+    for b in range(blocks):
+        spectra.append(jnp.dot(filtered[b], dft_ref[...], preferred_element_type=jnp.float32))
     for b in range(blocks):
         re, im = spectra[b][:, :LANES], spectra[b][:, LANES:]
         amp = jnp.sqrt(re * re + im * im)

time: 19.9 us -> 20 us (level)
  no operation moved by 1% of the time
where the time goes in v6:
time: 20 us; the launch traced here: 19.9 us
  starting transfers between devices  8.19 us (41%)
  waiting for transfers between devices  7.25 us (36%)
  Pallas kernels  4.42 us (22%)
    ppermute x6, starting transfers between devices, send(): lax.ppermute(value, axes, [(number[d], number[to(*d)]) for d in devices])  8.19 us
    ppermute x6, waiting for transfers between devices, send(): lax.ppermute(value, axes, [(number[d], number[to(*d)]) for d in devices])  7.25 us
    pallas_call x1, Pallas kernels, local_cross(): pl.pallas_call(spectra_kernel, out_shape=[jax.ShapeDtypeStruct((BLOCK * w...  3.31 us
    pallas_call x4, Pallas kernels, in_vmem(): pl.pallas_call(kernel, out_shape=out_shape, in_specs=[vmem] * len(inputs)...  1.11 us
  transfers between devices with their start and end apart: 6, of which 6 were waited for; matrix products, arithmetic and copies ran while one was open for 0% of the time, Pallas kernels for 0%

profile of v6, /device:TPU:0, one launch (start us, length us, event | category | flops | bytes accessed | tf_op | source)
XLA Modules:
  0.0 19.9 jit_solution(11352317093957804232)
XLA Ops:
  0.0 3.3 %shard_map.55 = (bf16[160,768]{1,0:T(8,128)(2,1)S(1)}, bf16[96,768]{1,0:T(8,128)(2,1)S(1)}) custom-call(s32[4]{0:T(128)} %ids_hbm.1, bf16[4,256,512]{2,1,0:T(8,128)(2,1)} %rec_hbm.1, f32[1,65]{1,0:T(1,128)} %bitcast.1, bf16[512,256]{1,0:T(8,128)(2,1)} %constant.4.clone.dft_hbm), custom_call_target="tpu_custom_call" | custom-call | tf_op jit(solution)/shard_map/pallas_call | solution.py:208
  3.3 0.5 %collective-permute-start = (bf16[160,768]{1,0:T(8,128)(2,1)S(1)}, bf16[160,768]{1,0:T(8,128)(2,1)S(1)}, u32[]{:S(2)}, u32[]{:S(2)}) collective-permute-start(bf16[160,768]{1,0:T(8,128)(2,1)S(1)} %get-tuple-element.11.own), channel_id=1, source_target_pairs={{0,1},{1,0},{2,3},{3,2},{4,5},{5,4},{6,7},{7,6},{8,9},{9,8},{10,11... | collective-permute-start | bytes 737288 | tf_op jit(solution)/shard_map/ppermute | solution.py:307
  3.8 1.1 %collective-permute-done.other = bf16[160,768]{1,0:T(8,128)(2,1)S(1)} collective-permute-done((bf16[160,768]{1,0:T(8,128)(2,1)S(1)}, bf16[160,768]{1,0:T(8,128)(2,1)S(1)}, u32[]{:S(2)}, u32[]{:S(2)}) %collective-permute-start) | collective-permute-done | bytes 245792 | tf_op jit(solution)/shard_map/ppermute | solution.py:307
  5.0 0.1 shard_map.56
  5.0 4.0 %collective-permute-start.1 = (bf16[32,768]{1,0:T(8,128)(2,1)S(1)}, bf16[32,768]{1,0:T(8,128)(2,1)S(1)}, u32[]{:S(2)}, u32[]{:S(2)}) collective-permute-start(bf16[32,768]{1,0:T(8,128)(2,1)S(1)} %get-tuple-element.14), channel_id=1, source_target_pairs={{0,8},{1,9},{2,10},{3,11},{4,12},{5,13},{6,14},{7,15},{8,0},{9,1},... | collective-permute-start | bytes 147464 | tf_op jit(solution)/shard_map/ppermute | solution.py:307
  9.1 1.3 %collective-permute-start.2 = (bf16[32,768]{1,0:T(8,128)(2,1)S(1)}, bf16[32,768]{1,0:T(8,128)(2,1)S(1)}, u32[]{:S(2)}, u32[]{:S(2)}) collective-permute-start(bf16[32,768]{1,0:T(8,128)(2,1)S(1)} %get-tuple-element.15), channel_id=1, source_target_pairs={{0,12},{1,13},{2,14},{3,15},{4,0},{5,1},{6,2},{7,3},{8,4},{9,5},{1... | collective-permute-start | bytes 147464 | tf_op jit(solution)/shard_map/ppermute | solution.py:307
  10.4 0.7 %collective-permute-start.4 = (bf16[64,768]{1,0:T(8,128)(2,1)S(1)}, bf16[64,768]{1,0:T(8,128)(2,1)S(1)}, u32[]{:S(2)}, u32[]{:S(2)}) collective-permute-start(bf16[64,768]{1,0:T(8,128)(2,1)S(1)} %get-tuple-element.16), channel_id=1, source_target_pairs={{0,4},{1,7},{2,6},{3,5},{4,8},{5,11},{6,10},{7,9},{8,12},{9,15},{1... | collective-permute-start | bytes 294920 | tf_op jit(solution)/shard_map/ppermute | solution.py:307
  11.1 0.1 collective-permute-done.1.refs_1_
  11.1 2.0 %collective-permute-done.2.refs_2_ = bf16[32,768]{1,0:T(8,128)(2,1)S(1)} collective-permute-done((bf16[32,768]{1,0:T(8,128)(2,1)S(1)}, bf16[32,768]{1,0:T(8,128)(2,1)S(1)}, u32[]{:S(2)}, u32[]{:S(2)}) %collective-permute-start.2) | collective-permute-done | bytes 49184 | tf_op jit(solution)/shard_map/ppermute | solution.py:307
  13.2 0.0 copy-start
  13.2 1.6 %collective-permute-start.3 = (bf16[32,768]{1,0:T(8,128)(2,1)S(1)}, bf16[32,768]{1,0:T(8,128)(2,1)S(1)}, u32[]{:S(2)}, u32[]{:S(2)}) collective-permute-start(bf16[32,768]{1,0:T(8,128)(2,1)S(1)} %shard_map.57.refs_0_), channel_id=1, source_target_pairs={{0,2},{1,3},{2,0},{3,1},{4,6},{5,7},{6,4},{7,5},{8,10},{9,11},{10,... | collective-permute-start | bytes 147464 | tf_op jit(solution)/shard_map/ppermute | solution.py:307
  14.7 2.6 %collective-permute-done.3.refs_1_ = bf16[32,768]{1,0:T(8,128)(2,1)S(1)} collective-permute-done((bf16[32,768]{1,0:T(8,128)(2,1)S(1)}, bf16[32,768]{1,0:T(8,128)(2,1)S(1)}, u32[]{:S(2)}, u32[]{:S(2)}) %collective-permute-start.3) | collective-permute-done | bytes 49184 | tf_op jit(solution)/shard_map/ppermute | solution.py:307
  17.3 0.1 collective-permute-done.4.refs_2_
  17.4 0.1 collective-permute-start.5
  17.5 1.4 %collective-permute-done.5.other = bf16[96,768]{1,0:T(8,128)(2,1)S(1)} collective-permute-done((bf16[96,768]{1,0:T(8,128)(2,1)S(1)}, bf16[96,768]{1,0:T(8,128)(2,1)S(1)}, u32[]{:S(2)}, u32[]{:S(2)}) %collective-permute-start.5) | collective-permute-done | bytes 147488 | tf_op jit(solution)/shard_map/ppermute | solution.py:307
  18.9 0.0 copy-done
  18.9 1.0 %shard_map.59 = f32[4,64,256]{2,1,0:T(8,128)} custom-call(bf16[512,256]{1,0:T(8,128)(2,1)S(1)} %copy-done, bf16[96,768]{1,0:T(8,128)(2,1)S(1)} %shard_map.58.own, bf16[96,768]{1,0:T(8,128)(2,1)S(1)} %collective-permute-done.5.other), custom_call_target="tpu_custom_call" | custom-call | tf_op jit(solution)/shard_map/pallas_call | solution.py:289
  (2 shorter events, 0.0 us)
Async XLA Ops:
  3.3 1.7 %collective-permute-start = (bf16[160,768]{1,0:T(8,128)(2,1)S(1)}, bf16[160,768]{1,0:T(8,128)(2,1)S(1)}, u32[]{:S(2)}, u32[]{:S(2)}) collective-permute-start(bf16[160,768]{1,0:T(8,128)(2,1)S(1)} %get-tuple-element.11.own), channel_id=1, source_target_pairs={{0,1},{1,0},{2,3},{3,2},{4,5},{5,4},{6,7},{7,6},{8,9},{9,8},{10,11... | collective-permute-start | bytes 737288 | tf_op jit(solution)/shard_map/ppermute | solution.py:307
  5.0 6.1 %collective-permute-start.1 = (bf16[32,768]{1,0:T(8,128)(2,1)S(1)}, bf16[32,768]{1,0:T(8,128)(2,1)S(1)}, u32[]{:S(2)}, u32[]{:S(2)}) collective-permute-start(bf16[32,768]{1,0:T(8,128)(2,1)S(1)} %get-tuple-element.14), channel_id=1, source_target_pairs={{0,8},{1,9},{2,10},{3,11},{4,12},{5,13},{6,14},{7,15},{8,0},{9,1},... | collective-permute-start | bytes 147464 | tf_op jit(solution)/shard_map/ppermute | solution.py:307
  9.1 4.1 %collective-permute-start.2 = (bf16[32,768]{1,0:T(8,128)(2,1)S(1)}, bf16[32,768]{1,0:T(8,128)(2,1)S(1)}, u32[]{:S(2)}, u32[]{:S(2)}) collective-permute-start(bf16[32,768]{1,0:T(8,128)(2,1)S(1)} %get-tuple-element.15), channel_id=1, source_target_pairs={{0,12},{1,13},{2,14},{3,15},{4,0},{5,1},{6,2},{7,3},{8,4},{9,5},{1... | collective-permute-start | bytes 147464 | tf_op jit(solution)/shard_map/ppermute | solution.py:307
  10.4 7.0 %collective-permute-start.4 = (bf16[64,768]{1,0:T(8,128)(2,1)S(1)}, bf16[64,768]{1,0:T(8,128)(2,1)S(1)}, u32[]{:S(2)}, u32[]{:S(2)}) collective-permute-start(bf16[64,768]{1,0:T(8,128)(2,1)S(1)} %get-tuple-element.16), channel_id=1, source_target_pairs={{0,4},{1,7},{2,6},{3,5},{4,8},{5,11},{6,10},{7,9},{8,12},{9,15},{1... | collective-permute-start | bytes 294920 | tf_op jit(solution)/shard_map/ppermute | solution.py:307
  13.2 5.7 %copy-start = (bf16[512,256]{1,0:T(8,128)(2,1)S(1)}, bf16[512,256]{1,0:T(8,128)(2,1)}, u32[]{:S(2)}) copy-start(bf16[512,256]{1,0:T(8,128)(2,1)} %constant.5.clone.table_ref) | copy-start | bytes 786436
  13.2 4.2 %collective-permute-start.3 = (bf16[32,768]{1,0:T(8,128)(2,1)S(1)}, bf16[32,768]{1,0:T(8,128)(2,1)S(1)}, u32[]{:S(2)}, u32[]{:S(2)}) collective-permute-start(bf16[32,768]{1,0:T(8,128)(2,1)S(1)} %shard_map.57.refs_0_), channel_id=1, source_target_pairs={{0,2},{1,3},{2,0},{3,1},{4,6},{5,7},{6,4},{7,5},{8,10},{9,11},{10,... | collective-permute-start | bytes 147464 | tf_op jit(solution)/shard_map/ppermute | solution.py:307
  17.4 1.4 %collective-permute-start.5 = (bf16[96,768]{1,0:T(8,128)(2,1)S(1)}, bf16[96,768]{1,0:T(8,128)(2,1)S(1)}, u32[]{:S(2)}, u32[]{:S(2)}) collective-permute-start(bf16[96,768]{1,0:T(8,128)(2,1)S(1)} %shard_map.58.own), channel_id=1, source_target_pairs={{0,1},{1,0},{2,3},{3,2},{4,5},{5,4},{6,7},{7,6},{8,9},{9,8},{10,11... | collective-permute-start | bytes 442376 | tf_op jit(solution)/shard_map/ppermute | solution.py:307

commit v7 on v6

--- a/solution.py
+++ b/solution.py
@@ -187,16 +187,21 @@
         start = width * len(whole) + half * i
         value = cross(k)
         top, bottom = value[:half], value[half:]
-        out_ref[start : start + half, :] = jnp.where(first, bottom, top)
-        kept_ref[half * i : half * (i + 1), :] = jnp.where(first, top, bottom)
+        upper = first if k else ~first
+        out_ref[start : start + half, :] = jnp.where(upper, bottom, top)
+        kept_ref[half * i : half * (i + 1), :] = jnp.where(upper, top, bottom)
 
 
 def kinds(blocks):
-    return list(range(1, blocks // 2)), list(range(blocks // 2, blocks)) + [0]
+    return list(range(3 * blocks // 4 - 1, 0, -1)), list(range(3 * blocks // 4, blocks)) + [0]
 
 
 def relative(me, k, size):
-    return (me + k) % size
+    half = size // 2
+    if k < half:
+        return me ^ k
+    low = (me < half) * 1
+    return low * (half + (me + k) % half) + (1 - low) * ((size - 1 - me + k) % half)
 
 
 def local_cross(source_ids, records, taps, dft):
@@ -271,7 +276,7 @@
     first = lax.axis_index("rep") == 0
     mine, theirs = own[rows:, :].astype(jnp.float32), other[rows:, :].astype(jnp.float32)
     shares = jnp.concatenate(
-        [jnp.where(first, mine, theirs), jnp.where(first, theirs, mine)], axis=0
+        [jnp.where(first, theirs, mine), jnp.where(first, mine, theirs)], axis=0
     )
     total = own[:rows, :].astype(jnp.float32) + other[:rows, :].astype(jnp.float32) + shares
     cross = unpack(total)
@@ -320,7 +325,7 @@
         [own, kept, other],
     )
     shares = [
-        send(piece, lambda a, t, r, k=k: (relative(a, k, chans), t, r))
+        send(piece, lambda a, t, r, k=k: (relative(a, k, chans), t, 1 - r))
         for k, piece in zip(shared[:-1], pieces[len(whole) :])
     ]
     arrived = [

time: 20 us -> 19.9 us (level)
  starting transfers between devices: 8.19 us -> 7.81 us
    ppermute x6, starting transfers between devices: 8.19 us -> 7.81 us  [send(): lax.ppermute(value, axes, [(number[d], number[to(*d)]) for d in devices])]
  transfers between devices with their start and end apart: 6 -> 6, of which waited for: 6 -> 4; matrix products, arithmetic and copies ran while one was open for 0% -> 0% of each run, Pallas kernels for 0% -> 0%
where the time goes in v7:
time: 19.9 us; the launch traced here: 19.7 us
  starting transfers between devices  7.81 us (39%)
  waiting for transfers between devices  7.44 us (37%)
  Pallas kernels  4.42 us (22%)
    ppermute x6, starting transfers between devices, send(): lax.ppermute(value, axes, [(number[d], number[to(*d)]) for d in devices])  7.81 us
    ppermute x6, waiting for transfers between devices, send(): lax.ppermute(value, axes, [(number[d], number[to(*d)]) for d in devices])  7.44 us
    pallas_call x1, Pallas kernels, local_cross(): pl.pallas_call(spectra_kernel, out_shape=[jax.ShapeDtypeStruct((BLOCK * w...  3.29 us
    pallas_call x4, Pallas kernels, in_vmem(): pl.pallas_call(kernel, out_shape=out_shape, in_specs=[vmem] * len(inputs)...  1.13 us
  transfers between devices with their start and end apart: 6, of which 4 were waited for; matrix products, arithmetic and copies ran while one was open for 0% of the time, Pallas kernels for 0%

profile of v7, /device:TPU:0, one launch (start us, length us, event | category | flops | bytes accessed | tf_op | source)
XLA Modules:
  0.0 19.7 jit_solution(17174162485519818838)
XLA Ops:
  0.0 3.3 %shard_map.55 = (bf16[192,768]{1,0:T(8,128)(2,1)S(1)}, bf16[64,768]{1,0:T(8,128)(2,1)S(1)}) custom-call(s32[4]{0:T(128)} %ids_hbm.1, bf16[4,256,512]{2,1,0:T(8,128)(2,1)} %rec_hbm.1, f32[1,65]{1,0:T(1,128)} %bitcast.1, bf16[512,256]{1,0:T(8,128)(2,1)} %constant.4.clone.dft_hbm), custom_call_target="tpu_custom_call" | custom-call | tf_op jit(solution)/shard_map/pallas_call | solution.py:213
  3.3 0.5 %collective-permute-start = (bf16[192,768]{1,0:T(8,128)(2,1)S(1)}, bf16[192,768]{1,0:T(8,128)(2,1)S(1)}, u32[]{:S(2)}, u32[]{:S(2)}) collective-permute-start(bf16[192,768]{1,0:T(8,128)(2,1)S(1)} %get-tuple-element.11.own), channel_id=1, source_target_pairs={{0,1},{1,0},{2,3},{3,2},{4,5},{5,4},{6,7},{7,6},{8,9},{9,8},{10,11... | collective-permute-start | bytes 884744 | tf_op jit(solution)/shard_map/ppermute | solution.py:312
  3.8 1.2 %collective-permute-done.other = bf16[192,768]{1,0:T(8,128)(2,1)S(1)} collective-permute-done((bf16[192,768]{1,0:T(8,128)(2,1)S(1)}, bf16[192,768]{1,0:T(8,128)(2,1)S(1)}, u32[]{:S(2)}, u32[]{:S(2)}) %collective-permute-start) | collective-permute-done | bytes 294944 | tf_op jit(solution)/shard_map/ppermute | solution.py:312
  5.0 0.1 shard_map.56
  5.1 4.8 %collective-permute-start.1 = (bf16[32,768]{1,0:T(8,128)(2,1)S(1)}, bf16[32,768]{1,0:T(8,128)(2,1)S(1)}, u32[]{:S(2)}, u32[]{:S(2)}) collective-permute-start(bf16[32,768]{1,0:T(8,128)(2,1)S(1)} %get-tuple-element.14), channel_id=1, source_target_pairs={{0,13},{1,12},{2,15},{3,14},{4,9},{5,8},{6,11},{7,10},{8,1},{9,0},... | collective-permute-start | bytes 147464 | tf_op jit(solution)/shard_map/ppermute | solution.py:312
  9.9 0.0 collective-permute-start.3
  9.9 0.9 %collective-permute-start.4 = (bf16[64,768]{1,0:T(8,128)(2,1)S(1)}, bf16[64,768]{1,0:T(8,128)(2,1)S(1)}, u32[]{:S(2)}, u32[]{:S(2)}) collective-permute-start(bf16[64,768]{1,0:T(8,128)(2,1)S(1)} %get-tuple-element.16), channel_id=1, source_target_pairs={{0,4},{1,7},{2,6},{3,5},{4,0},{5,3},{6,2},{7,1},{8,12},{9,15},{10,... | collective-permute-start | bytes 294920 | tf_op jit(solution)/shard_map/ppermute | solution.py:312
  10.8 1.3 %collective-permute-done.1.refs_1_ = bf16[32,768]{1,0:T(8,128)(2,1)S(1)} collective-permute-done((bf16[32,768]{1,0:T(8,128)(2,1)S(1)}, bf16[32,768]{1,0:T(8,128)(2,1)S(1)}, u32[]{:S(2)}, u32[]{:S(2)}) %collective-permute-start.1) | collective-permute-done | bytes 49184 | tf_op jit(solution)/shard_map/ppermute | solution.py:312
  12.0 0.0 copy-start
  12.1 1.6 %collective-permute-start.2 = (bf16[32,768]{1,0:T(8,128)(2,1)S(1)}, bf16[32,768]{1,0:T(8,128)(2,1)S(1)}, u32[]{:S(2)}, u32[]{:S(2)}) collective-permute-start(bf16[32,768]{1,0:T(8,128)(2,1)S(1)} %shard_map.57.refs_0_), channel_id=1, source_target_pairs={{0,2},{1,3},{2,0},{3,1},{4,6},{5,7},{6,4},{7,5},{8,10},{9,11},{10,... | collective-permute-start | bytes 147464 | tf_op jit(solution)/shard_map/ppermute | solution.py:312
  13.6 3.6 %collective-permute-done.2.refs_1_ = bf16[32,768]{1,0:T(8,128)(2,1)S(1)} collective-permute-done((bf16[32,768]{1,0:T(8,128)(2,1)S(1)}, bf16[32,768]{1,0:T(8,128)(2,1)S(1)}, u32[]{:S(2)}, u32[]{:S(2)}) %collective-permute-start.2) | collective-permute-done | bytes 49184 | tf_op jit(solution)/shard_map/ppermute | solution.py:312
  17.2 0.0 collective-permute-done.3.refs_2_
  17.2 0.0 collective-permute-done.4.refs_3_
  17.3 0.1 collective-permute-start.5
  17.3 1.4 %collective-permute-done.5.other = bf16[96,768]{1,0:T(8,128)(2,1)S(1)} collective-permute-done((bf16[96,768]{1,0:T(8,128)(2,1)S(1)}, bf16[96,768]{1,0:T(8,128)(2,1)S(1)}, u32[]{:S(2)}, u32[]{:S(2)}) %collective-permute-start.5) | collective-permute-done | bytes 147488 | tf_op jit(solution)/shard_map/ppermute | solution.py:312
  18.7 0.0 copy-done
  18.7 1.0 %shard_map.59 = f32[4,64,256]{2,1,0:T(8,128)} custom-call(bf16[512,256]{1,0:T(8,128)(2,1)S(1)} %copy-done, bf16[96,768]{1,0:T(8,128)(2,1)S(1)} %shard_map.58.own, bf16[96,768]{1,0:T(8,128)(2,1)S(1)} %collective-permute-done.5.other), custom_call_target="tpu_custom_call" | custom-call | tf_op jit(solution)/shard_map/pallas_call | solution.py:294
  (2 shorter events, 0.1 us)
Async XLA Ops:
  3.3 1.7 %collective-permute-start = (bf16[192,768]{1,0:T(8,128)(2,1)S(1)}, bf16[192,768]{1,0:T(8,128)(2,1)S(1)}, u32[]{:S(2)}, u32[]{:S(2)}) collective-permute-start(bf16[192,768]{1,0:T(8,128)(2,1)S(1)} %get-tuple-element.11.own), channel_id=1, source_target_pairs={{0,1},{1,0},{2,3},{3,2},{4,5},{5,4},{6,7},{7,6},{8,9},{9,8},{10,11... | collective-permute-start | bytes 884744 | tf_op jit(solution)/shard_map/ppermute | solution.py:312
  5.1 6.9 %collective-permute-start.1 = (bf16[32,768]{1,0:T(8,128)(2,1)S(1)}, bf16[32,768]{1,0:T(8,128)(2,1)S(1)}, u32[]{:S(2)}, u32[]{:S(2)}) collective-permute-start(bf16[32,768]{1,0:T(8,128)(2,1)S(1)} %get-tuple-element.14), channel_id=1, source_target_pairs={{0,13},{1,12},{2,15},{3,14},{4,9},{5,8},{6,11},{7,10},{8,1},{9,0},... | collective-permute-start | bytes 147464 | tf_op jit(solution)/shard_map/ppermute | solution.py:312
  9.9 7.4 %collective-permute-start.3 = (bf16[64,768]{1,0:T(8,128)(2,1)S(1)}, bf16[64,768]{1,0:T(8,128)(2,1)S(1)}, u32[]{:S(2)}, u32[]{:S(2)}) collective-permute-start(bf16[64,768]{1,0:T(8,128)(2,1)S(1)} %get-tuple-element.15), channel_id=1, source_target_pairs={{0,8},{1,11},{2,10},{3,9},{4,12},{5,15},{6,14},{7,13},{8,4},{9,7},... | collective-permute-start | bytes 294920 | tf_op jit(solution)/shard_map/ppermute | solution.py:312
  9.9 7.4 %collective-permute-start.4 = (bf16[64,768]{1,0:T(8,128)(2,1)S(1)}, bf16[64,768]{1,0:T(8,128)(2,1)S(1)}, u32[]{:S(2)}, u32[]{:S(2)}) collective-permute-start(bf16[64,768]{1,0:T(8,128)(2,1)S(1)} %get-tuple-element.16), channel_id=1, source_target_pairs={{0,4},{1,7},{2,6},{3,5},{4,0},{5,3},{6,2},{7,1},{8,12},{9,15},{10,... | collective-permute-start | bytes 294920 | tf_op jit(solution)/shard_map/ppermute | solution.py:312
  12.0 6.7 %copy-start = (bf16[512,256]{1,0:T(8,128)(2,1)S(1)}, bf16[512,256]{1,0:T(8,128)(2,1)}, u32[]{:S(2)}) copy-start(bf16[512,256]{1,0:T(8,128)(2,1)} %constant.5.clone.table_ref) | copy-start | bytes 786436
  12.1 5.2 %collective-permute-start.2 = (bf16[32,768]{1,0:T(8,128)(2,1)S(1)}, bf16[32,768]{1,0:T(8,128)(2,1)S(1)}, u32[]{:S(2)}, u32[]{:S(2)}) collective-permute-start(bf16[32,768]{1,0:T(8,128)(2,1)S(1)} %shard_map.57.refs_0_), channel_id=1, source_target_pairs={{0,2},{1,3},{2,0},{3,1},{4,6},{5,7},{6,4},{7,5},{8,10},{9,11},{10,... | collective-permute-start | bytes 147464 | tf_op jit(solution)/shard_map/ppermute | solution.py:312
  17.3 1.4 %collective-permute-start.5 = (bf16[96,768]{1,0:T(8,128)(2,1)S(1)}, bf16[96,768]{1,0:T(8,128)(2,1)S(1)}, u32[]{:S(2)}, u32[]{:S(2)}) collective-permute-start(bf16[96,768]{1,0:T(8,128)(2,1)S(1)} %shard_map.58.own), channel_id=1, source_target_pairs={{0,1},{1,0},{2,3},{3,2},{4,5},{5,4},{6,7},{7,6},{8,9},{9,8},{10,11... | collective-permute-start | bytes 442376 | tf_op jit(solution)/shard_map/ppermute | solution.py:312
